TPU v7x, 32 devices: a whole 2x2x4 slice. The times are simulated.
32 devices in a mesh: dp: 4 (over y, x), ctx: 8 (over z, core).
Axes of the slice: x: 2, y: 2, z: 4, core: 2. Of those that a mesh axis runs over, the one named last changes fastest.
Arguments:
- tokens: bfloat16 [4, 4096, 1024], P('dp', 'ctx'), may hold values from -6 to 6
- starts: int32 [4, 512], P('dp', 'ctx'), may hold values from 0 to 4095, as said below
- gain: float32 [1024], replicated, may hold values from 0.1 to 1.9
- w_query: bfloat16 [1024, 1024], P('dp')
- w_key: bfloat16 [1024, 1024], P('dp')
- w_value: bfloat16 [1024, 1024], P('dp'), may hold values from -0.1875 to 0.1875
- w_out: bfloat16 [1024, 1024], P('dp'), may hold values from -0.1875 to 0.1875
- cotangent: bfloat16 [4, 4096, 1024], P('dp', 'ctx'), may hold values from -6 to 6
Outputs:
- grad_tokens: bfloat16 [4, 4096, 1024], P('dp', 'ctx')
Inputs may be any that keep to these rules, and one draw needn't show every extreme that they name: starts[b, 0] is 0 and starts[b, j] rises strictly with j; segment j lies with the device that holds starts[b, j], and every position held by one device along ctx belongs to a segment held by that device or by one of its two neighbours along ctx; in the first sequence segment 64 - 1 starts at 513 or later and the last segment starts at 4095.
All inputs are finite; a program needn't handle non-finite values.
Results may differ from a plain program's by a relative error of at most 0.013.
Values may be sent and summed in bfloat16 or wider, within the bound.
A program may use at most 128 MiB of HBM per device.

v0:
```python
import math

import jax
import jax.numpy as jnp
from jax import lax
from jax.sharding import PartitionSpec as P

HEAD = 128


def padded(cells, sides, width):
    for axis, dim in sides:
        count = lax.axis_size(axis)
        ends = count - 1
        head = lax.slice_in_dim(cells, 0, width, axis=dim)
        tail = lax.slice_in_dim(cells, cells.shape[dim] - width, cells.shape[dim], axis=dim)
        cells = jnp.concatenate(
            [
                lax.ppermute(tail, axis, [(i, (i + 1) % count) for i in range(ends)]),
                cells,
                lax.ppermute(head, axis, [((i + 1) % count, i) for i in range(ends)]),
            ],
            axis=dim,
        )
    return cells


def from_behind(value, axis, steps):
    count = lax.axis_size(axis)
    leading, last = (max(0, -steps), min(count, count - steps))
    return lax.ppermute(value, axis, [(source, source + steps) for source in range(leading, last)])


def contract_last(left, right):
    return lax.dot_general(
        left, right, (((1,), (1,)), ((), ())), preferred_element_type=jnp.float32
    )


def contract_first(left, right):
    return lax.dot_general(
        left, right, (((0,), (0,)), ((), ())), preferred_element_type=jnp.float32
    )


def per_device(tokens, starts, gain, w_query, w_key, w_value, w_out, cotangent):
    inner = w_query.shape[1]
    heads = inner // HEAD
    scale = 1.0 / math.sqrt(HEAD)
    token_rows = tokens[0]
    grad_out = cotangent[0]
    own_starts = starts[0]
    rows = token_rows.shape[0]
    seg_dev = own_starts.shape[0]
    ctx_count = lax.axis_size("ctx")
    ctx_place = lax.axis_index("ctx")
    positions = ctx_place * rows + lax.iota(jnp.int32, rows)
    start_window = padded(own_starts, (("ctx", 0),), seg_dev)
    window_slot = lax.iota(jnp.int32, 3 * seg_dev)
    missing_left = (ctx_place == 0) & (window_slot < seg_dev)
    missing_right = (ctx_place == ctx_count - 1) & (window_slot >= 2 * seg_dev)
    start_window = jnp.where(missing_left, -1, start_window)
    start_window = jnp.where(missing_right, rows * ctx_count, start_window)
    local_seg = jnp.sum((start_window[None, :] <= positions[:, None]).astype(jnp.int32), axis=1) - 1
    member = local_seg[:, None] == window_slot[None, :]
    earlier_member = (local_seg - 1)[:, None] == window_slot[None, :]
    window_sum = contract_first(member.astype(jnp.bfloat16), token_rows)
    window_grad = contract_first(earlier_member.astype(jnp.bfloat16), grad_out)
    window_count = jnp.sum(member.astype(jnp.float32), axis=0)
    lower = slice(0, seg_dev)
    middle = slice(seg_dev, 2 * seg_dev)
    upper = slice(2 * seg_dev, 3 * seg_dev)
    from_after = from_behind(
        (window_sum[lower], window_grad[lower], window_count[lower]), "ctx", -1
    )
    from_before = (
        from_behind(window_sum[upper].astype(jnp.bfloat16), "ctx", 1).astype(jnp.float32),
        from_behind(window_grad[upper].astype(jnp.bfloat16), "ctx", 1).astype(jnp.float32),
        from_behind(window_count[upper].astype(jnp.bfloat16), "ctx", 1).astype(jnp.float32),
    )
    count = window_count[middle] + from_after[2] + from_before[2]
    pooled = (window_sum[middle] + from_after[0] + from_before[0]) / count[:, None]
    dout = window_grad[middle] + from_after[1] + from_before[1]
    rms = jnp.sqrt(jnp.mean(pooled * pooled, axis=-1, keepdims=True) + 1e-06)
    normed = pooled / rms
    normin = (normed * gain).astype(jnp.bfloat16)
    dout_b = dout.astype(jnp.bfloat16)
    full_q, full_k, full_v, full_o = (
        lax.all_gather(w_query, "dp", axis=0, tiled=True),
        lax.all_gather(w_key, "dp", axis=0, tiled=True),
        lax.all_gather(w_value, "dp", axis=0, tiled=True),
        lax.all_gather(w_out, "dp", axis=0, tiled=True),
    )
    query = jnp.dot(normin, full_q, preferred_element_type=jnp.float32).astype(jnp.bfloat16)
    keys = jnp.dot(normin, full_k, preferred_element_type=jnp.float32).astype(jnp.bfloat16)
    values = jnp.dot(normin, full_v, preferred_element_type=jnp.float32).astype(jnp.bfloat16)
    dattended = contract_last(dout_b, full_o).astype(jnp.bfloat16)
    key_all, value_all = (
        lax.all_gather(keys, "ctx", axis=0, tiled=True),
        lax.all_gather(values, "ctx", axis=0, tiled=True),
    )
    total = key_all.shape[0]
    seg_iota = lax.iota(jnp.int32, seg_dev)
    query3 = query.reshape(seg_dev, heads, HEAD)
    key3 = key_all.reshape(total, heads, HEAD)
    value3 = value_all.reshape(total, heads, HEAD)
    dattended3 = dattended.reshape(seg_dev, heads, HEAD)
    query_place = ctx_place * seg_dev + seg_iota
    allowed = lax.iota(jnp.int32, total)[None, :] <= query_place[:, None]
    score = jnp.einsum("qhd,khd->hqk", query3, key3, preferred_element_type=jnp.float32) * scale
    score = jnp.where(allowed[None], score, -1e30)
    peak = jnp.max(score, axis=-1, keepdims=True)
    expo = jnp.where(allowed[None], jnp.exp(score - peak), 0.0)
    expo_total = jnp.sum(expo, axis=-1, keepdims=True)
    probs = expo / expo_total
    probs_b = probs.astype(jnp.bfloat16)
    attended3 = jnp.einsum(
        "hqk,khd->qhd", probs_b, value3, preferred_element_type=jnp.float32
    ).astype(jnp.bfloat16)
    delta = jnp.einsum("qhd,qhd->hq", dattended3.astype(jnp.float32), attended3.astype(jnp.float32))
    dprobs = jnp.einsum("qhd,khd->hqk", dattended3, value3, preferred_element_type=jnp.float32)
    dscore = (probs * (dprobs - delta[:, :, None])).astype(jnp.bfloat16)
    dquery = (
        (jnp.einsum("hqk,khd->qhd", dscore, key3, preferred_element_type=jnp.float32) * scale)
        .astype(jnp.bfloat16)
        .reshape(seg_dev, inner)
    )
    dkey_part = (
        jnp.einsum("hqk,qhd->khd", dscore, query3, preferred_element_type=jnp.float32) * scale
    )
    dvalue_part = jnp.einsum(
        "hqk,qhd->khd", probs_b, dattended3, preferred_element_type=jnp.float32
    )
    key_grad = lax.psum_scatter(
        jnp.concatenate(
            [
                dkey_part.reshape(lax.axis_size("ctx") * seg_dev, inner),
                dvalue_part.reshape(lax.axis_size("ctx") * seg_dev, inner),
            ],
            axis=1,
        ).astype(jnp.bfloat16),
        "ctx",
        scatter_dimension=0,
        tiled=True,
    ).astype(jnp.float32)
    dkey = key_grad[:, :inner].astype(jnp.bfloat16)
    dvalue = key_grad[:, inner:].astype(jnp.bfloat16)
    dnormin = (
        contract_last(dquery, full_q) + contract_last(dkey, full_k) + contract_last(dvalue, full_v)
    )
    scaled = dnormin * gain
    dpooled = dout + (scaled - normed * jnp.mean(scaled * normed, axis=-1, keepdims=True)) / rms
    per_seg = dpooled / count[:, None]
    per_window = padded(per_seg.astype(jnp.bfloat16), (("ctx", 0),), seg_dev).astype(per_seg.dtype)
    spread = jnp.dot(member.astype(jnp.float32), per_window, precision=lax.Precision.HIGHEST)
    result = grad_out.astype(jnp.float32) + spread
    return result.astype(jnp.bfloat16)[None]


def solution(mesh):
    return jax.shard_map(
        per_device,
        mesh=mesh,
        in_specs=(
            P("dp", "ctx", None),
            P("dp", "ctx"),
            P(),
            P("dp", None),
            P("dp", None),
            P("dp", None),
            P("dp", None),
            P("dp", "ctx", None),
        ),
        out_specs=P("dp", "ctx", None),
        check_vma=False,
    )
```

profile of v0, /device:TPU:1, one launch (start us, length us, event | category | flops | bytes accessed | tf_op | source)
XLA Modules:
  0.0 268.5 jit_solution(1486526116337268122)
XLA Ops:
  6.5 0.7 all-gather.7.cloned.1.call-update
  7.3 0.0 all-gather.15.cloned.1.call-start
  7.3 0.7 all-gather.15.cloned.1.call-update
  8.0 0.0 all-gather.13.cloned.1.call-start
  8.1 0.7 all-gather.13.cloned.1.call-update
  8.8 0.0 all-gather.11.cloned.1.call-start
  8.8 0.5 all-gather.11.cloned.1.call-update
  9.4 2.0 collective-permute-start.1
  11.4 4.5 %collective-permute-start = (s32[64]{0:T(128)S(1)}, s32[64]{0:T(128)S(1)}, u32[]{:S(2)}, u32[]{:S(2)}) collective-permute-start(s32[64]{0:T(128)S(1)} %bitcast.100), channel_id=1, source_target_pairs={{0,1},{1,2},{2,3},{3,4},{4,5},{5,6},{6,7},{8,9},{9,10},{10,11},{11... | collective-permute-start | bytes 776 | tf_op jit(solution)/shard_map/ppermute | solution.py:19
  16.0 0.7 collective-permute-done
  16.6 0.1 and_select_fusion.1
  16.7 0.1 convert_reduce_fusion.1
  16.8 0.4 fusion.20
  17.2 1.9 collective-permute-start.4
  19.2 0.1 convert_reduce_fusion
  19.3 1.9 collective-permute-start.6
  21.3 4.2 %collective-permute-start.7 = (bf16[64]{0:T(256)(128)(2,1)S(1)}, bf16[64]{0:T(256)(128)(2,1)S(1)}, u32[]{:S(2)}, u32[]{:S(2)}) collective-permute-start(bf16[64]{0:T(256)(128)(2,1)S(1)} %slice.46), channel_id=1, source_target_pairs={{0,1},{1,2},{2,3},{3,4},{4,5},{5,6},{6,7},{8,9},{9,10},{10,11},{11... | collective-permute-start | bytes 392 | tf_op jit(solution)/shard_map/ppermute | solution.py:31
  25.4 2.4 collective-permute-start.5
  27.9 0.1 convert_add_fusion
  28.0 1.8 collective-permute-done.5
  29.8 0.2 multiply_reduce_fusion.1
  30.0 0.6 add_sqrt_fusion
  30.6 0.1 multiply_convert_fusion.1
  30.7 15.9 %all-gather.7.cloned.1.call-done = bf16[1024,1024]{1,0:T(8,128)(2,1)} async-done(((bf16[256,1024]{1,0:T(8,128)(2,1)}), bf16[1024,1024]{1,0:T(8,128)(2,1)}) %all-gather.7.cloned.1.call-update) | async-done | bytes 2097168 | tf_op jit(solution)/shard_map/all_gather | solution.py:90
  46.6 2.7 %convolution_convert_fusion.4 = bf16[64,1024]{1,0:T(8,128)(2,1)} fusion(bf16[64,1024]{1,0:T(8,128)(2,1)S(1)} %get-tuple-element.5, bf16[1024,1024]{1,0:T(8,128)(2,1)} %all-gather.7.cloned.1.call-done), kind=kOutput, calls=%fused_computation.21 | convolution fusion | flops 134283264 | bytes 2359296 | tf_op jit(solution)/shard_map/dot_general | solution.py:95
  49.4 0.0 all-gather.17.cloned.1.call-start
  49.4 0.6 fusion.22
  50.1 2.6 collective-permute-start.2
  52.6 31.2 %all-gather.15.cloned.1.call-done = bf16[1024,1024]{1,0:T(8,128)(2,1)} async-done(((bf16[256,1024]{1,0:T(8,128)(2,1)}), bf16[1024,1024]{1,0:T(8,128)(2,1)}) %all-gather.15.cloned.1.call-update) | async-done | bytes 2097168 | tf_op jit(solution)/shard_map/all_gather | solution.py:91
  83.8 2.7 %convolution_convert_fusion.1 = bf16[64,1024]{1,0:T(8,128)(2,1)} fusion(bf16[64,1024]{1,0:T(8,128)(2,1)S(1)} %get-tuple-element.5, bf16[1024,1024]{1,0:T(8,128)(2,1)} %all-gather.15.cloned.1.call-done), kind=kOutput, calls=%fused_computation.18 | convolution fusion | flops 134283264 | bytes 2359296 | tf_op jit(solution)/shard_map/dot_general | solution.py:96
  86.6 0.0 reduce-scatter.4.cloned.1.call-start
  86.7 3.7 %collective-permute-start.3 = (bf16[64,1024]{1,0:T(8,128)(2,1)S(1)}, bf16[64,1024]{1,0:T(8,128)(2,1)S(1)}, u32[]{:S(2)}, u32[]{:S(2)}) collective-permute-start(bf16[64,1024]{1,0:T(8,128)(2,1)S(1)} %slice.80), channel_id=1, source_target_pairs={{0,1},{1,2},{2,3},{3,4},{4,5},{5,6},{6,7},{8,9},{9,10},{10,11},{11... | collective-permute-start | bytes 393224 | tf_op jit(solution)/shard_map/ppermute | solution.py:31
  90.3 0.1 iota_compare_fusion.5
  90.4 1.8 collective-permute-done.3
  92.3 28.7 %all-gather.13.cloned.1.call-done = bf16[1024,1024]{1,0:T(8,128)(2,1)} async-done(((bf16[256,1024]{1,0:T(8,128)(2,1)}), bf16[1024,1024]{1,0:T(8,128)(2,1)}) %all-gather.13.cloned.1.call-update) | async-done | bytes 2097168 | tf_op jit(solution)/shard_map/all_gather | solution.py:92
  121.0 2.3 convolution_convert_fusion.2
  123.4 0.6 copy-done.9
  124.1 34.0 %all-gather.11.cloned.1.call-done = bf16[1024,1024]{1,0:T(8,128)(2,1)} async-done(((bf16[256,1024]{1,0:T(8,128)(2,1)}), bf16[1024,1024]{1,0:T(8,128)(2,1)}) %all-gather.11.cloned.1.call-update) | async-done | bytes 2097168 | tf_op jit(solution)/shard_map/all_gather | solution.py:89
  158.1 2.1 fusion.10
  160.1 0.7 bitcast_convert_fusion
  160.9 21.1 %all-gather.9.cloned.1.call-done = bf16[512,1024]{1,0:T(8,128)(2,1)} async-done(((bf16[64,1024]{1,0:T(8,128)(2,1)}), bf16[512,1024]{1,0:T(8,128)(2,1)}) %all-gather.9.cloned.1.call-update) | async-done | bytes 1048592 | tf_op jit(solution)/shard_map/all_gather | solution.py:99
  182.0 1.7 fusion.5
  183.8 1.1 fusion.58
  184.9 3.0 %convolution_convert_fusion = bf16[8,128,512]{2,1,0:T(8,128)(2,1)} fusion(f32[8,64]{1,0:T(8,128)S(1)} %get-tuple-element.11, f32[8,64,512]{2,1,0:T(8,128)S(1)} %fusion.5, pred[64,512]{1,0:T(8,128)(4,1)} %copy-done.14, bf16[64,1024]{1,0:T(8,128)(2,1)} %copy-done.9), kind=kOutput, calls=%fused_computation.5 | convolution fusion | flops 68682752 | bytes 2263040 | tf_op jit(solution)/shard_map/hqk,qhd->khd/dot_general | solution.py:131
  187.9 17.4 %all-gather.17.cloned.1.call-done = bf16[512,1024]{1,0:T(8,128)(2,1)} async-done(((bf16[64,1024]{1,0:T(8,128)(2,1)}), bf16[512,1024]{1,0:T(8,128)(2,1)}) %all-gather.17.cloned.1.call-update) | async-done | bytes 1048592 | tf_op jit(solution)/shard_map/all_gather | solution.py:100
  205.2 3.0 %fusion.14 = f32[8,64]{1,0:T(8,128)} fusion(f32[8,64,128]{2,0,1:T(8,128)} %bitcast_convert_fusion, f32[8,64]{1,0:T(8,128)S(1)} %get-tuple-element.11, f32[8,64,512]{2,1,0:T(8,128)S(1)} %fusion.5, pred[64,512]{1,0:T(8,128)(4,1)} %copy-done.14, bf16[512,1024]{1,0:T(8,128)(2,1)} %all-gather.17.cloned.1.call-done), kind=kOutput, calls=%fused_computation.28 | convolution fusion | flops 68420096 | bytes 2396160 | tf_op jit(solution)/shard_map/hqk,khd->qhd/dot_general | solution.py:117
  208.3 1.7 fusion.7
  210.0 0.5 multiply_convert_fusion
  210.5 0.3 copy-done.10
  210.8 0.6 copy-done.6
  211.4 0.1 pad_maximum_fusion
  211.5 2.5 copy.48
  214.1 1.2 copy-done.5
  215.3 0.1 copy-done.11
  215.4 0.3 fusion.15
  215.7 3.2 %fusion.39 = f32[64,1024]{1,0:T(8,128)} fusion(bf16[1024,1024]{1,0:T(8,128)(2,1)} %all-gather.11.cloned.1.call-done, bf16[8,8,8,128]{3,2,1,0:T(8,128)(2,1)S(1)} %fusion.15), kind=kOutput, calls=%fused_computation.66 | convolution fusion | flops 134217728 | bytes 2490368 | tf_op jit(solution)/shard_map/dot_general | solution.py:35
  218.9 27.6 %reduce-scatter.4.cloned.1.call-done = bf16[64,2048]{1,0:T(8,128)(2,1)} async-done(((bf16[512,2048]{1,0:T(8,128)(2,1)}), bf16[64,2048]{1,0:T(8,128)(2,1)}) %reduce-scatter.4.cloned.1.call-update) | async-done | bytes 262160
  246.6 2.4 convolution_add_fusion.1
  249.1 0.9 multiply_reduce_fusion
  250.0 1.1 divide_convert_fusion
  251.1 5.2 %collective-permute-start.9 = (bf16[64,1024]{1,0:T(8,128)(2,1)S(1)}, bf16[64,1024]{1,0:T(8,128)(2,1)S(1)}, u32[]{:S(2)}, u32[]{:S(2)}) collective-permute-start(bf16[64,1024]{1,0:T(8,128)(2,1)S(1)} %divide_convert_fusion), channel_id=1, source_target_pairs={{1,0},{2,1},{3,2},{4,3},{5,4},{6,5},{7,6},{9,8},{10,9},{11,10},{12... | collective-permute-start | bytes 393224 | tf_op jit(solution)/shard_map/ppermute | solution.py:21
  256.3 1.9 collective-permute-start.8
  258.2 1.9 collective-permute-done.8
  260.2 1.5 fusion.6
  (56 shorter events, 0.3 us)
Async XLA Ops:
  6.5 10.3 %copy-start = (bf16[1,512,1024]{2,1,0:T(8,128)(2,1)S(1)}, bf16[1,512,1024]{2,1,0:T(8,128)(2,1)}, u32[]{:S(2)}) copy-start(bf16[1,512,1024]{2,1,0:T(8,128)(2,1)} %param.8) | copy-start | bytes 3145732
  6.5 2.8 %copy-start.18 = (s32[1,64]{1,0:T(1,128)S(1)}, s32[1,64]{1,0:T(1,128)}, u32[]{:S(2)}) copy-start(s32[1,64]{1,0:T(1,128)} %param.9) | copy-start | bytes 772
  6.5 40.1 %all-gather.7.cloned.1.call-start = ((), (), s32[]{:S(2)}) async-start(), calls=%async_computation.1 | async-start | bytes 2621440 | tf_op jit(solution)/shard_map/all_gather | solution.py:90
  7.3 76.6 %all-gather.15.cloned.1.call-start = ((), (), s32[]{:S(2)}) async-start(), calls=%async_computation.5 | async-start | bytes 2621440 | tf_op jit(solution)/shard_map/all_gather | solution.py:91
  8.0 22.6 %copy-start.16 = (f32[1024]{0:T(1024)S(1)}, f32[1024]{0:T(1024)}, u32[]{:S(2)}) copy-start(f32[1024]{0:T(1024)} %param.10) | copy-start | bytes 12292
  8.0 113.0 %all-gather.13.cloned.1.call-start = ((), (), s32[]{:S(2)}) async-start(), calls=%async_computation.4 | async-start | bytes 2621440 | tf_op jit(solution)/shard_map/all_gather | solution.py:92
  8.8 149.3 %all-gather.11.cloned.1.call-start = ((), (), s32[]{:S(2)}) async-start(), calls=%async_computation.3 | async-start | bytes 2621440 | tf_op jit(solution)/shard_map/all_gather | solution.py:89
  9.3 172.7 %all-gather.9.cloned.1.call-start = ((), (), s32[]{:S(2)}) async-start(), calls=%async_computation.2 | async-start | bytes 1179648 | tf_op jit(solution)/shard_map/all_gather | solution.py:99
  9.4 6.6 %collective-permute-start.1 = (s32[64]{0:T(128)S(1)}, s32[64]{0:T(128)S(1)}, u32[]{:S(2)}, u32[]{:S(2)}) collective-permute-start(s32[64]{0:T(128)S(1)} %bitcast.99), channel_id=1, source_target_pairs={{1,0},{2,1},{3,2},{4,3},{5,4},{6,5},{7,6},{9,8},{10,9},{11,10},{12... | collective-permute-start | bytes 776 | tf_op jit(solution)/shard_map/ppermute | solution.py:21
  11.4 5.3 %collective-permute-start = (s32[64]{0:T(128)S(1)}, s32[64]{0:T(128)S(1)}, u32[]{:S(2)}, u32[]{:S(2)}) collective-permute-start(s32[64]{0:T(128)S(1)} %bitcast.100), channel_id=1, source_target_pairs={{0,1},{1,2},{2,3},{3,4},{4,5},{5,6},{6,7},{8,9},{9,10},{10,11},{11... | collective-permute-start | bytes 776 | tf_op jit(solution)/shard_map/ppermute | solution.py:19
  17.2 12.5 %collective-permute-start.4 = (f32[64,1024]{1,0:T(8,128)S(1)}, f32[64,1024]{1,0:T(8,128)S(1)}, u32[]{:S(2)}, u32[]{:S(2)}) collective-permute-start(f32[64,1024]{1,0:T(8,128)S(1)} %slice.53), channel_id=1, source_target_pairs={{1,0},{2,1},{3,2},{4,3},{5,4},{6,5},{7,6},{9,8},{10,9},{11,10},{12... | collective-permute-start | bytes 786440 | tf_op jit(solution)/shard_map/ppermute | solution.py:31
  19.3 8.6 %collective-permute-start.6 = (f32[64]{0:T(128)S(1)}, f32[64]{0:T(128)S(1)}, u32[]{:S(2)}, u32[]{:S(2)}) collective-permute-start(f32[64]{0:T(128)S(1)} %slice.45), channel_id=1, source_target_pairs={{1,0},{2,1},{3,2},{4,3},{5,4},{6,5},{7,6},{9,8},{10,9},{11,10},{12... | collective-permute-start | bytes 776 | tf_op jit(solution)/shard_map/ppermute | solution.py:31
  21.3 6.6 %collective-permute-start.7 = (bf16[64]{0:T(256)(128)(2,1)S(1)}, bf16[64]{0:T(256)(128)(2,1)S(1)}, u32[]{:S(2)}, u32[]{:S(2)}) collective-permute-start(bf16[64]{0:T(256)(128)(2,1)S(1)} %slice.46), channel_id=1, source_target_pairs={{0,1},{1,2},{2,3},{3,4},{4,5},{5,6},{6,7},{8,9},{9,10},{10,11},{11... | collective-permute-start | bytes 392 | tf_op jit(solution)/shard_map/ppermute | solution.py:31
  25.4 4.3 %collective-permute-start.5 = (bf16[64,1024]{1,0:T(8,128)(2,1)S(1)}, bf16[64,1024]{1,0:T(8,128)(2,1)S(1)}, u32[]{:S(2)}, u32[]{:S(2)}) collective-permute-start(bf16[64,1024]{1,0:T(8,128)(2,1)S(1)} %slice.79), channel_id=1, source_target_pairs={{0,1},{1,2},{2,3},{3,4},{4,5},{5,6},{6,7},{8,9},{9,10},{10,11},{11... | collective-permute-start | bytes 393224 | tf_op jit(solution)/shard_map/ppermute | solution.py:31
  28.0 21.5 %copy-start.3 = (bf16[1,512,1024]{2,1,0:T(8,128)(2,1)S(1)}, bf16[1,512,1024]{2,1,0:T(8,128)(2,1)}, u32[]{:S(2)}) copy-start(bf16[1,512,1024]{2,1,0:T(8,128)(2,1)} %param.15) | copy-start | bytes 3145732
  49.4 155.9 %all-gather.17.cloned.1.call-start = ((), (), s32[]{:S(2)}) async-start(), calls=%async_computation.6 | async-start | bytes 1179648 | tf_op jit(solution)/shard_map/all_gather | solution.py:100
  50.0 73.3 %copy-start.2 = (f32[192,1024]{1,0:T(8,128)}, f32[192,1024]{1,0:T(8,128)S(1)}, u32[]{:S(2)}) copy-start(f32[192,1024]{1,0:T(8,128)S(1)} %fusion.22) | copy-start | bytes 2359300
  50.1 42.2 %collective-permute-start.2 = (f32[64,1024]{1,0:T(8,128)S(1)}, f32[64,1024]{1,0:T(8,128)S(1)}, u32[]{:S(2)}, u32[]{:S(2)}) collective-permute-start(f32[64,1024]{1,0:T(8,128)S(1)} %slice.50), channel_id=1, source_target_pairs={{1,0},{2,1},{3,2},{4,3},{5,4},{6,5},{7,6},{9,8},{10,9},{11,10},{12... | collective-permute-start | bytes 786440 | tf_op jit(solution)/shard_map/ppermute | solution.py:31
  86.6 160.0 %reduce-scatter.4.cloned.1.call-start = ((), (), s32[]{:S(2)}) async-start(), calls=%async_computation.7 | async-start | bytes 2359296
  86.7 5.6 %collective-permute-start.3 = (bf16[64,1024]{1,0:T(8,128)(2,1)S(1)}, bf16[64,1024]{1,0:T(8,128)(2,1)S(1)}, u32[]{:S(2)}, u32[]{:S(2)}) collective-permute-start(bf16[64,1024]{1,0:T(8,128)(2,1)S(1)} %slice.80), channel_id=1, source_target_pairs={{0,1},{1,2},{2,3},{3,4},{4,5},{5,6},{6,7},{8,9},{9,10},{10,11},{11... | collective-permute-start | bytes 393224 | tf_op jit(solution)/shard_map/ppermute | solution.py:31
  90.4 91.6 %copy-start.14 = (pred[64,512]{1,0:T(8,128)(4,1)}, pred[64,512]{1,0:T(8,128)(4,1)S(1)}, u32[]{:S(2)}) copy-start(pred[64,512]{1,0:T(8,128)(4,1)S(1)} %iota_compare_fusion.5) | copy-start | bytes 98308
  92.3 67.9 %copy-start.12 = (bf16[64,1024]{1,0:T(8,128)(2,1)}, bf16[64,1024]{1,0:T(8,128)(2,1)S(1)}, u32[]{:S(2)}) copy-start(bf16[64,1024]{1,0:T(8,128)(2,1)S(1)} %collective-permute-done.3) | copy-start | bytes 393220
  92.3 31.8 %copy-start.7 = (f32[64,1024]{1,0:T(8,128)}, f32[64,1024]{1,0:T(8,128)S(1)}, u32[]{:S(2)}) copy-start(f32[64,1024]{1,0:T(8,128)S(1)} %collective-permute-done.2) | copy-start | bytes 786436
  123.4 0.7 copy-start.9
  210.0 0.8 copy-start.10
  210.0 1.4 copy-start.6
  214.0 1.2 copy-start.5
  214.0 1.4 copy-start.11
  215.7 33.3 %copy-start.1 = (bf16[1024,1024]{1,0:T(8,128)(2,1)S(1)}, bf16[1024,1024]{1,0:T(8,128)(2,1)}, u32[]{:S(2)}) copy-start(bf16[1024,1024]{1,0:T(8,128)(2,1)} %all-gather.15.cloned.1.call-done) | copy-start | bytes 6291460
  246.6 2.5 copy-start.15
  249.0 1.0 copy-start.8
  249.0 1.0 copy-start.13
  249.0 1.0 copy-start.17
  249.0 11.1 %copy-start.4 = (bf16[1,512,1024]{2,1,0:T(8,128)(2,1)S(1)}, bf16[1,512,1024]{2,1,0:T(8,128)(2,1)}, u32[]{:S(2)}) copy-start(bf16[1,512,1024]{2,1,0:T(8,128)(2,1)} %param.15) | copy-start | bytes 3145732
  251.1 7.2 %collective-permute-start.9 = (bf16[64,1024]{1,0:T(8,128)(2,1)S(1)}, bf16[64,1024]{1,0:T(8,128)(2,1)S(1)}, u32[]{:S(2)}, u32[]{:S(2)}) collective-permute-start(bf16[64,1024]{1,0:T(8,128)(2,1)S(1)} %divide_convert_fusion), channel_id=1, source_target_pairs={{1,0},{2,1},{3,2},{4,3},{5,4},{6,5},{7,6},{9,8},{10,9},{11,10},{12... | collective-permute-start | bytes 393224 | tf_op jit(solution)/shard_map/ppermute | solution.py:21
  256.3 3.9 %collective-permute-start.8 = (bf16[64,1024]{1,0:T(8,128)(2,1)S(1)}, bf16[64,1024]{1,0:T(8,128)(2,1)S(1)}, u32[]{:S(2)}, u32[]{:S(2)}) collective-permute-start(bf16[64,1024]{1,0:T(8,128)(2,1)S(1)} %divide_convert_fusion), channel_id=1, source_target_pairs={{0,1},{1,2},{2,3},{3,4},{4,5},{5,6},{6,7},{8,9},{9,10},{10,11},{11... | collective-permute-start | bytes 393224 | tf_op jit(solution)/shard_map/ppermute | solution.py:19
Sparse Core Ops, SparseCore 0:
  9.2 37.3 all-gather.6
  48.5 35.2 all-gather.14
  85.7 35.2 all-gather.12
  122.7 35.2 all-gather.10
  159.5 22.4 all-gather.8
  183.5 21.7 all-gather.16
  214.2 32.3 reduce-scatter.3
where the time goes:
time: 269 us; the launch traced here: 268 us
  waiting for transfers between devices  185 us (69%)
  starting transfers between devices  30.5 us (11%)
  matrix products  29 us (11%)
  between operations  13.9 us (5%)
  local copies, waits for them, and re-layouts  5.58 us (2%)
  other arithmetic  4.47 us (2%)
    all_gather x1, waiting for transfers between devices, per_device(): lax.all_gather(w_query, 'dp', axis=0, tiled=True)  34 us
    all_gather x1, waiting for transfers between devices, per_device(): lax.all_gather(w_value, 'dp', axis=0, tiled=True)  31.2 us
    unnamed x8, waiting for transfers between devices  30.3 us
    all_gather x1, waiting for transfers between devices, per_device(): lax.all_gather(w_out, 'dp', axis=0, tiled=True)  28.7 us
    all_gather x1, waiting for transfers between devices, per_device(): lax.all_gather(keys, 'ctx', axis=0, tiled=True)  21.1 us
    all_gather x1, waiting for transfers between devices, per_device(): lax.all_gather(values, 'ctx', axis=0, tiled=True)  17.4 us
    ppermute x6, starting transfers between devices, from_behind(): lax.ppermute(value, axis, [(source, source + steps) for source in range(l...  16.7 us
    all_gather x1, waiting for transfers between devices, per_device(): lax.all_gather(w_key, 'dp', axis=0, tiled=True)  15.9 us
  transfers between devices with their start and end apart: 17, of which 11 were waited for; matrix products, arithmetic and copies ran while one was open for 8% of the time, Pallas kernels for 0%

commit v1 on v0

v1 whole, which is shorter than its diff:
```python
import functools
import math

import jax
import jax.numpy as jnp
from jax import lax
from jax.experimental import pallas as pl
from jax.experimental.pallas import tpu as pltpu
from jax.sharding import PartitionSpec as P

HEAD = 128
BF = jnp.bfloat16
F32 = jnp.float32


def dot(left, right, dims):
    return lax.dot_general(left, right, ((dims[0], dims[1]), ((), ())), preferred_element_type=F32)


def mm(left, right):
    return dot(left, right, ((1,), (0,)))


def mm_nt(left, right):
    return dot(left, right, ((1,), (1,)))


def mm_tn(left, right):
    return dot(left, right, ((0,), (0,)))


def remote(src, dst, send, recv, **where):
    return pltpu.make_async_remote_copy(
        src_ref=src, dst_ref=dst, send_sem=send, recv_sem=recv,
        device_id=where, device_id_type=pl.DeviceIdType.MESH,
    )


def kernel(
    n, dp,
    tok, starts, gain, wq, wk, wv, wo, cot, out,
    st_mine, st_near, near_out, near_in, gath, wcat, wout, qkv, datt, dqkv, dkv,
    part, sib, red, rs, seg_out, seg_in, member_s,
    st_send, st_recv, near_send, near_recv, seg_send, seg_recv,
    w_send, w_recv, w_local, wo_send, wo_recv, wo_local,
    right_send, left_send, pair_send, gath_recv, sib_send, sib_recv, rs_send, rs_recv,
):
    me = lax.axis_index("dp")
    c = lax.axis_index("ctx")
    core = lax.rem(c, 2)
    chip = lax.div(c, 2)
    chips = n // 2
    mate = c + 1 - 2 * core
    rows = tok.shape[1]
    width = tok.shape[2]
    seg_dev = starts.shape[1]
    segs = n * seg_dev
    w_rows = wq.shape[0]
    inner = wq.shape[1]
    heads = inner // HEAD
    parts = n // heads
    h = lax.rem(c, heads)
    r = lax.div(c, heads)
    scale = 1.0 / math.sqrt(HEAD)
    has_prev, has_next = c > 0, c < n - 1

    barrier = pltpu.get_barrier_semaphore()
    for o in range(1, n):
        pl.semaphore_signal(barrier, inc=1, device_id={"ctx": lax.rem(c + o, n)},
                            device_id_type=pl.DeviceIdType.MESH)
    for o in range(1, dp):
        pl.semaphore_signal(barrier, inc=1, device_id={"dp": lax.rem(me + o, dp)},
                            device_id_type=pl.DeviceIdType.MESH)
    st_mine[...] = jnp.zeros_like(st_mine)
    st_mine[0:1, 0:seg_dev] = starts[...]
    pl.semaphore_wait(barrier, n - 1 + dp - 1)

    def to_next(src, dst, send, recv):
        return remote(src, dst.at[0], send.at[0], recv.at[0], ctx=c + 1)

    def to_prev(src, dst, send, recv):
        return remote(src, dst.at[1], send.at[1], recv.at[1], ctx=c - 1)

    def near_start(src_next, src_prev, dst, send, recv):
        @pl.when(has_next)
        def _():
            to_next(src_next, dst, send, recv).start()

        @pl.when(has_prev)
        def _():
            to_prev(src_prev, dst, send, recv).start()

    def near_wait(src_next, src_prev, dst, send, recv):
        @pl.when(has_prev)
        def _():
            to_next(src_next, dst, send, recv).wait_recv()
            to_prev(src_prev, dst, send, recv).wait_send()

        @pl.when(has_next)
        def _():
            to_prev(src_prev, dst, send, recv).wait_recv()
            to_next(src_next, dst, send, recv).wait_send()

    near_start(st_mine, st_mine, st_near, st_send, st_recv)

    head_at = pl.multiple_of(h * HEAD, HEAD)
    mats = (wq, wk, wv)

    def w_copy(o, i):
        mine = pl.ds(pl.multiple_of(me * w_rows, w_rows), w_rows)
        return remote(mats[i].at[:, pl.ds(head_at, HEAD)], wcat.at[mine, pl.ds(i * HEAD, HEAD)],
                      w_send.at[o - 1, i], w_recv.at[o - 1, i], dp=lax.rem(me + o, dp))

    def w_arrival(o, i):
        src = lax.rem(me + dp - o, dp)
        theirs = pl.ds(pl.multiple_of(src * w_rows, w_rows), w_rows)
        return remote(mats[i].at[:, pl.ds(head_at, HEAD)], wcat.at[theirs, pl.ds(i * HEAD, HEAD)],
                      w_send.at[o - 1, i], w_recv.at[o - 1, i], dp=lax.rem(me + o, dp))

    def w_own(i):
        mine = pl.ds(pl.multiple_of(me * w_rows, w_rows), w_rows)
        return pltpu.make_async_copy(mats[i].at[:, pl.ds(head_at, HEAD)],
                                     wcat.at[mine, pl.ds(i * HEAD, HEAD)], w_local.at[i])

    holder = lax.div(h * HEAD, w_rows)
    holder_at = pl.ds(pl.multiple_of(lax.rem(h * HEAD, w_rows), HEAD), HEAD)

    def wo_copy(o):
        return remote(wo.at[holder_at], wout, wo_send.at[o - 1], wo_recv.at[0],
                      dp=lax.rem(me + o, dp))

    for o in range(1, dp):
        for i in range(3):
            w_copy(o, i).start()
    for i in range(3):
        w_own(i).start()

    @pl.when(me == holder)
    def _():
        for o in range(1, dp):
            wo_copy(o).start()
        pltpu.make_async_copy(wo.at[holder_at], wout, wo_local.at[0]).start()

    near_wait(st_mine, st_mine, st_near, st_send, st_recv)
    own_row = starts[...].astype(F32)
    prev_row = jnp.where(has_prev, st_near[0, 0:1, 0:seg_dev].astype(F32), -1.0)
    next_row = jnp.where(has_next, st_near[1, 0:1, 0:seg_dev].astype(F32), float(rows * n))
    sub = lax.broadcasted_iota(jnp.int32, (seg_dev, seg_dev), 0)
    lane = lax.broadcasted_iota(jnp.int32, (seg_dev, seg_dev), 1)

    def column(mask, row):
        return jnp.sum(jnp.where(mask, row, 0.0), axis=1, keepdims=True)

    def follow(row, after):
        edge = (sub == seg_dev - 1) & (lane == 0)
        return column(lane == sub + 1, row) + column(edge, after)

    same = lane == sub
    pos = (lax.broadcasted_iota(jnp.int32, (1, rows), 1) + c * rows).astype(F32)
    own_col, own_end = column(same, own_row), follow(own_row, next_row)
    end_row = jnp.full((1, seg_dev), float(rows * n), F32)

    def belongs(first, last):
        return jnp.where((first <= pos) & (pos < last), 1.0, 0.0).astype(BF)

    member_s[0:seg_dev] = belongs(column(same, prev_row), follow(prev_row, own_row))
    member_s[seg_dev:2 * seg_dev] = belongs(own_col, own_end)
    member_s[2 * seg_dev:] = belongs(column(same, next_row), follow(next_row, end_row))

    for side, at in ((1, 0), (0, 2 * seg_dev)):
        some = member_s[at:at + seg_dev]
        near_out[side, :, 0:width] = mm(some, tok[0]).astype(BF)
        near_out[side, :, width:] = mm(some, cot[0]).astype(BF)
    near_start(near_out.at[0], near_out.at[1], near_in, near_send, near_recv)
    some = member_s[seg_dev:2 * seg_dev]
    sum_tok = mm(some, tok[0])
    sum_cot = mm(some, cot[0])

    @pl.when(jnp.logical_not(has_prev))
    def _():
        near_in[0] = jnp.zeros_like(near_in[0])

    @pl.when(jnp.logical_not(has_next))
    def _():
        near_in[1] = jnp.zeros_like(near_in[1])

    near_wait(near_out.at[0], near_out.at[1], near_in, near_send, near_recv)

    def spot(k, where):
        return gath.at[k, pl.ds(pl.multiple_of(where * seg_dev, seg_dev), seg_dev)]

    def hop(k, src_chip, sems, **where):
        at = 2 * src_chip + core
        return remote(spot(k, at), spot(k, at), sems.at[k, src_chip], gath_recv.at[k, at], **where)

    def go_right(k, src):
        return hop(k, src, right_send, ctx=c + 2)

    def go_left(k, src):
        return hop(k, src, left_send, ctx=c - 2)

    def go_pair(k, src):
        return hop(k, src, pair_send, ctx=mate)

    def arrival(k, where):
        return remote(spot(k, where), spot(k, where), right_send.at[k, 0], gath_recv.at[k, where],
                      ctx=mate)

    not_last, not_first = chip < chips - 1, chip > 0

    def launch(k):
        @pl.when(not_last)
        def _():
            go_right(k, chip).start()

        @pl.when(not_first)
        def _():
            go_left(k, chip).start()

        go_pair(k, chip).start()

    own_at = pl.ds(pl.multiple_of(c * seg_dev, seg_dev), seg_dev)
    grad_sum = sum_cot + near_in[0, :, width:].astype(F32) + near_in[1, :, width:].astype(F32)
    gath[0, own_at] = grad_sum.astype(BF)
    launch(0)
    count = own_end - own_col
    pooled = (sum_tok + near_in[0, :, 0:width].astype(F32) + near_in[1, :, 0:width].astype(F32)) / count
    rms = jnp.sqrt(jnp.mean(pooled * pooled, axis=-1, keepdims=True) + 1e-06)
    normed = pooled / rms
    gath[1, own_at] = (normed * gain[...]).astype(BF)
    launch(1)

    for s in range(1, chips):
        for k in range(2):
            @pl.when(chip - s >= 0)
            def _():
                arrival(k, c - 2 * s).wait_recv()

                @pl.when(not_last)
                def _():
                    go_right(k, chip - s).start()

                go_pair(k, chip - s).start()

            @pl.when(chip + s < chips)
            def _():
                arrival(k, c + 2 * s).wait_recv()

                @pl.when(not_first)
                def _():
                    go_left(k, chip + s).start()

                go_pair(k, chip + s).start()

    for o in range(1, dp):
        for i in range(3):
            w_arrival(o, i).wait_recv()
    for i in range(3):
        w_own(i).wait()

    @pl.when(me == holder)
    def _():
        pltpu.make_async_copy(wo.at[holder_at], wout, wo_local.at[0]).wait()

    @pl.when(me != holder)
    def _():
        wo_copy(1).wait_recv()

    for k in range(2):
        for other in range(chips):
            arrival(k, 2 * other + 1 - core).wait_recv()

    step = 512 if segs % 512 == 0 else seg_dev

    def project(b, _):
        at = pl.ds(pl.multiple_of(b * step, step), step)
        qkv[at] = mm(gath[1, at], wcat[...]).astype(BF)
        datt[at] = mm_nt(gath[0, at], wout[...])
        return 0

    lax.fori_loop(0, segs // step, project, 0)
    shifted = pltpu.roll(datt[...], segs - 1, 0)
    last = lax.broadcasted_iota(jnp.int32, (segs, HEAD), 0) == segs - 1
    datt[...] = jnp.where(last, 0.0, shifted)

    dkv[...] = jnp.zeros_like(dkv)
    if parts > 1:
        dqkv[...] = jnp.zeros_like(dqkv)
    block = 128

    def attend(q_at, first, klen):
        q = qkv[q_at, 0:HEAD]
        key = qkv[0:klen, HEAD:2 * HEAD]
        value = qkv[0:klen, 2 * HEAD:]
        grad = datt[q_at].astype(BF)
        score = mm_nt(q, key) * scale
        allowed = (lax.broadcasted_iota(jnp.int32, (block, klen), 1)
                   <= lax.broadcasted_iota(jnp.int32, (block, klen), 0) + first)
        score = jnp.where(allowed, score, -1e30)
        peak = jnp.max(score, axis=-1, keepdims=True)
        expo = jnp.where(allowed, jnp.exp(score - peak), 0.0)
        probs = expo / jnp.sum(expo, axis=-1, keepdims=True)
        probs_b = probs.astype(BF)
        attended = mm(probs_b, value).astype(BF).astype(F32)
        delta = jnp.sum(grad.astype(F32) * attended, axis=-1, keepdims=True)
        dscore = (probs * (mm_nt(grad, value) - delta)).astype(BF)
        dqkv[q_at, 0:HEAD] = (mm(dscore, key) * scale).astype(BF)
        dkv[0:klen, 0:HEAD] += mm_tn(dscore, q)
        dkv[0:klen, HEAD:] += mm_tn(probs_b, grad)

    per = segs // parts // block
    if parts == 1:
        for b in range(per):
            attend(slice(b * block, (b + 1) * block), b * block, (b + 1) * block)
    else:
        def body(b, _):
            first = pl.multiple_of((r * per + b) * block, block)
            attend(pl.ds(first, block), first, segs)
            return 0

        lax.fori_loop(0, per, body, 0)
    dqkv[:, HEAD:2 * HEAD] = (dkv[:, 0:HEAD] * scale).astype(BF)
    dqkv[:, 2 * HEAD:] = dkv[:, HEAD:].astype(BF)

    def sib_copy(t):
        return remote(part.at[1 - core, t], sib.at[t], sib_send.at[t], sib_recv.at[t], ctx=mate)

    def rs_copy(t):
        return remote(red.at[t], rs.at[chip], rs_send.at[t], rs_recv.at[chip], ctx=2 * t + core)

    def rs_arrival(t):
        return remote(red.at[t], rs.at[t], rs_send.at[t], rs_recv.at[t], ctx=mate)

    for t in range(chips):
        term = mm_nt(dqkv[2 * t * seg_dev:2 * (t + 1) * seg_dev], wcat[...])
        part[0, t] = term[0:seg_dev].astype(BF)
        part[1, t] = term[seg_dev:].astype(BF)
        sib_copy(t).start()
    for t in range(chips):
        sib_copy(t).wait_recv()
        red[t] = (part[core, t].astype(F32) + sib[t].astype(F32)).astype(BF)

        @pl.when(chip != t)
        def _():
            rs_copy(t).start()
    dnormin = red[chip].astype(F32)
    for o in range(1, chips):
        t = lax.rem(chip + o, chips)
        rs_arrival(t).wait_recv()
        dnormin = dnormin + rs[t].astype(F32)

    after = gath[0, pl.ds(pl.multiple_of(lax.rem(c + 1, n) * seg_dev, seg_dev), seg_dev)].astype(F32)
    tail = jnp.where(has_next, after[0:1], 0.0)
    rolled = pltpu.roll(grad_sum, seg_dev - 1, 0)
    ends = lax.broadcasted_iota(jnp.int32, (seg_dev, width), 0) == seg_dev - 1
    dout = jnp.where(ends, tail, rolled)
    scaled = dnormin * gain[...]
    dpooled = dout + (scaled - normed * jnp.mean(scaled * normed, axis=-1, keepdims=True)) / rms
    seg_out[...] = (dpooled / count).astype(BF)
    near_start(seg_out, seg_out, seg_in, seg_send, seg_recv)

    @pl.when(jnp.logical_not(has_prev))
    def _():
        seg_in[0] = jnp.zeros_like(seg_in[0])

    @pl.when(jnp.logical_not(has_next))
    def _():
        seg_in[1] = jnp.zeros_like(seg_in[1])

    for k in range(2):
        for other in range(chips):
            @pl.when(not_last & (other <= chip))
            def _():
                go_right(k, other).wait_send()

            @pl.when(not_first & (other >= chip))
            def _():
                go_left(k, other).wait_send()

            go_pair(k, other).wait_send()
    for t in range(chips):
        sib_copy(t).wait_send()

        @pl.when(chip != t)
        def _():
            rs_copy(t).wait_send()
    for o in range(1, dp):
        for i in range(3):
            w_copy(o, i).wait_send()

    @pl.when(me == holder)
    def _():
        for o in range(1, dp):
            wo_copy(o).wait_send()

    near_wait(seg_out, seg_out, seg_in, seg_send, seg_recv)
    window = jnp.concatenate([seg_in[0], seg_out[...], seg_in[1]], axis=0)
    spread = mm_tn(member_s[...], window)
    out[0] = (cot[0].astype(F32) + spread).astype(BF)


def per_device(tokens, starts, gain, w_query, w_key, w_value, w_out, cotangent):
    n, dp = lax.axis_size("ctx"), lax.axis_size("dp")
    chips = n // 2
    rows, width = tokens.shape[1:]
    seg_dev = starts.shape[1]
    segs = n * seg_dev
    dma = pltpu.SemaphoreType.DMA
    vmem = pltpu.VMEM
    scratch = [
        vmem((8, 128), jnp.int32),
        vmem((2, 8, 128), jnp.int32),
        vmem((2, seg_dev, 2 * width), BF),
        vmem((2, seg_dev, 2 * width), BF),
        vmem((2, segs, width), BF),
        vmem((width, 3 * HEAD), BF),
        vmem((HEAD, width), BF),
        vmem((segs, 3 * HEAD), BF),
        vmem((segs, HEAD), F32),
        vmem((segs, 3 * HEAD), BF),
        vmem((segs, 2 * HEAD), F32),
        vmem((2, chips, seg_dev, width), BF),
        vmem((chips, seg_dev, width), BF),
        vmem((chips, seg_dev, width), BF),
        vmem((chips, seg_dev, width), BF),
        vmem((seg_dev, width), BF),
        vmem((2, seg_dev, width), BF),
        vmem((3 * seg_dev, rows), BF),
        dma((2,)), dma((2,)), dma((2,)), dma((2,)), dma((2,)), dma((2,)),
        dma((dp - 1, 3)), dma((dp - 1, 3)), dma((3,)), dma((dp - 1,)), dma((1,)), dma((1,)),
        dma((2, chips)), dma((2, chips)), dma((2, chips)), dma((2, n)),
        dma((chips,)), dma((chips,)), dma((chips,)), dma((chips,)),
    ]
    return pl.pallas_call(
        functools.partial(kernel, n, dp),
        out_shape=jax.ShapeDtypeStruct(tokens.shape, BF),
        in_specs=[pl.BlockSpec(memory_space=pltpu.VMEM)] * 8,
        out_specs=pl.BlockSpec(memory_space=pltpu.VMEM),
        scratch_shapes=scratch,
        compiler_params=pltpu.CompilerParams(
            collective_id=0, has_side_effects=True, vmem_limit_bytes=56 * 1024 * 1024
        ),
    )(tokens, starts, gain[None], w_query, w_key, w_value, w_out, cotangent)


def solution(mesh):
    return jax.shard_map(
        per_device,
        mesh=mesh,
        in_specs=(
            P("dp", "ctx", None),
            P("dp", "ctx"),
            P(),
            P("dp", None),
            P("dp", None),
            P("dp", None),
            P("dp", None),
            P("dp", "ctx", None),
        ),
        out_specs=P("dp", "ctx", None),
        check_vma=False,
    )
```

time: 269 us -> 58.9 us (0.22)
  the two profiles are of different devices: /device:TPU:1 before, /device:TPU:17 now
where the time goes in v1:
time: 58.9 us; the launch traced here: 58.7 us
  Pallas kernels  56.5 us (96%)
  local copies, waits for them, and re-layouts  2.26 us (4%)
    pallas_call x1, Pallas kernels, per_device(): pl.pallas_call(functools.partial(kernel, n, dp), out_shape=jax.ShapeDtype...  56.5 us
    unnamed x1, local copies, waits for them, and re-layouts  2.26 us

profile of v1, /device:TPU:17, one launch (start us, length us, event | category | flops | bytes accessed | tf_op | source)
XLA Modules:
  0.0 58.7 jit_solution(10597995025004322445)
XLA Ops:
  0.0 56.5 %shard_map.82 = bf16[1,512,1024]{2,1,0:T(8,128)(2,1)} custom-call(bf16[1,512,1024]{2,1,0:T(8,128)(2,1)} %tok.1, s32[1,64]{1,0:T(1,128)} %starts.1, f32[1,1024]{1,0:T(1,128)} %bitcast.1, bf16[256,1024]{1,0:T(8,128)(2,1)} %wq.1, bf16[256,1024]{1,0:T(8,128)(2,1)} %wk.1, bf16[256,1024]{1,0:T(8,128)(2,1)} %wv.1, bf16[256,1024]{1,0:T(8,128)(2,1)} %wo.1, ...), custom_call_target="tpu_custom_call" | custom-call | tf_op jit(solution)/shard_map/pallas_call | solution.py:434
  56.5 2.3 %copy.10 = bf16[1,512,1024]{2,1,0:T(8,128)(2,1)} copy(bf16[1,512,1024]{2,1,0:T(8,128)(2,1)} %shard_map.82) | data formatting | bytes 2097152

commit v2 on v1

v2 whole, which is shorter than its diff:
```python
import functools
import math

import jax
import jax.numpy as jnp
from jax import lax
from jax.experimental import pallas as pl
from jax.experimental.pallas import tpu as pltpu
from jax.sharding import PartitionSpec as P

HEAD = 128
BF = jnp.bfloat16
F32 = jnp.float32


def dot(left, right, dims):
    return lax.dot_general(left, right, ((dims[0], dims[1]), ((), ())), preferred_element_type=F32)


def mm(left, right):
    return dot(left, right, ((1,), (0,)))


def mm_nt(left, right):
    return dot(left, right, ((1,), (1,)))


def mm_tn(left, right):
    return dot(left, right, ((0,), (0,)))


def remote(src, dst, send, recv, **where):
    return pltpu.make_async_remote_copy(
        src_ref=src, dst_ref=dst, send_sem=send, recv_sem=recv,
        device_id=where, device_id_type=pl.DeviceIdType.MESH,
    )


def kernel(
    n, dp,
    tok_hbm, starts, gain, wq, wk, wv, wo, cot_hbm, window, member,
    tok, cot, st_mine, st_near, near_out, near_in, head_out, head_in, gath, wcat, wout, grads, datt,
    qkv, dqkv, dkv, part, sib, red, rs, seg_out, seg_in,
    in_sem, st_send, st_recv, near_send, near_recv, head_send, head_recv, seg_send, seg_recv,
    w_send, w_recv, w_local, wo_send, wo_recv, wo_local, wo_fsend, wo_frecv,
    right_send, left_send, pair_send, gath_recv, datt_send, datt_recv,
    sib_send, sib_recv, rs_send, rs_recv,
):
    me = lax.axis_index("dp")
    c = lax.axis_index("ctx")
    core = lax.rem(c, 2)
    chip = lax.div(c, 2)
    chips = n // 2
    mate = c + 1 - 2 * core
    rows, width = tok.shape
    seg_dev = starts.shape[1]
    segs = n * seg_dev
    w_rows, inner = wq.shape
    half = w_rows // 2
    heads = inner // HEAD
    parts = n // heads
    h = lax.rem(c, heads)
    r = lax.div(c, heads)
    scale = 1.0 / math.sqrt(HEAD)
    has_prev, has_next = c > 0, c < n - 1

    barrier = pltpu.get_barrier_semaphore()
    for o in range(1, n):
        pl.semaphore_signal(barrier, inc=1, device_id={"ctx": lax.rem(c + o, n)},
                            device_id_type=pl.DeviceIdType.MESH)
    for o in range(1, dp):
        pl.semaphore_signal(barrier, inc=1, device_id={"dp": lax.rem(me + o, dp)},
                            device_id_type=pl.DeviceIdType.MESH)

    def dp_rows(where, extra=0, size=w_rows):
        return pl.ds(pl.multiple_of(where * w_rows + extra, size), size)

    cot_load = pltpu.make_async_copy(cot_hbm.at[0], cot, in_sem.at[0])
    tok_load = pltpu.make_async_copy(tok_hbm.at[0], tok, in_sem.at[1])
    head_at = pl.ds(pl.multiple_of(h * HEAD, HEAD), HEAD)
    mats = (wq, wk, wv)
    own_loads = [
        pltpu.make_async_copy(mats[i].at[:, head_at], wcat.at[dp_rows(me), pl.ds(i * HEAD, HEAD)],
                              w_local.at[i])
        for i in range(3)
    ]
    own_loads.append(pltpu.make_async_copy(wo, wout.at[dp_rows(me)], wo_local.at[0]))
    cot_load.start()
    tok_load.start()
    for load in own_loads:
        load.start()
    st_mine[...] = jnp.zeros_like(st_mine)
    st_mine[0:1, 0:seg_dev] = starts[...]
    pl.semaphore_wait(barrier, n - 1 + dp - 1)

    def to_next(src, dst, send, recv):
        return remote(src, dst.at[0], send.at[0], recv.at[0], ctx=c + 1)

    def to_prev(src, dst, send, recv):
        return remote(src, dst.at[1], send.at[1], recv.at[1], ctx=c - 1)

    def near_start(src_next, src_prev, dst, send, recv):
        @pl.when(has_next)
        def _():
            to_next(src_next, dst, send, recv).start()

        @pl.when(has_prev)
        def _():
            to_prev(src_prev, dst, send, recv).start()

    def near_wait(src_next, src_prev, dst, send, recv):
        @pl.when(has_prev)
        def _():
            to_next(src_next, dst, send, recv).wait_recv()
            to_prev(src_prev, dst, send, recv).wait_send()

        @pl.when(has_next)
        def _():
            to_prev(src_prev, dst, send, recv).wait_recv()
            to_next(src_next, dst, send, recv).wait_send()

    def near_clear(dst):
        @pl.when(jnp.logical_not(has_prev))
        def _():
            dst[0] = jnp.zeros_like(dst[0])

        @pl.when(jnp.logical_not(has_next))
        def _():
            dst[1] = jnp.zeros_like(dst[1])

    near_start(st_mine, st_mine, st_near, st_send, st_recv)

    def wo_copy(o):
        return remote(wo.at[pl.ds(pl.multiple_of(core * half, half), half)],
                      wout.at[dp_rows(me, core * half, half)],
                      wo_send.at[o - 1], wo_recv.at[o - 1], dp=lax.rem(me + o, dp))

    def wo_arrival(o, which, sends, recvs):
        at = dp_rows(lax.rem(me + dp - o, dp), which * half, half)
        return remote(wout.at[at], wout.at[at], sends.at[o - 1], recvs.at[o - 1], ctx=mate)

    for o in range(1, dp):
        wo_copy(o).start()

    def w_copy(o, i):
        return remote(mats[i].at[:, head_at], wcat.at[dp_rows(me), pl.ds(i * HEAD, HEAD)],
                      w_send.at[o - 1, i], w_recv.at[o - 1, i], dp=lax.rem(me + o, dp))

    def w_arrival(o, i):
        src = lax.rem(me + dp - o, dp)
        return remote(mats[i].at[:, head_at], wcat.at[dp_rows(src), pl.ds(i * HEAD, HEAD)],
                      w_send.at[o - 1, i], w_recv.at[o - 1, i], dp=lax.rem(me + o, dp))

    near_wait(st_mine, st_mine, st_near, st_send, st_recv)
    own_row = starts[...].astype(F32)
    prev_row = jnp.where(has_prev, st_near[0, 0:1, 0:seg_dev].astype(F32), -1.0)
    next_row = jnp.where(has_next, st_near[1, 0:1, 0:seg_dev].astype(F32), float(rows * n))
    sub = lax.broadcasted_iota(jnp.int32, (seg_dev, seg_dev), 0)
    lane = lax.broadcasted_iota(jnp.int32, (seg_dev, seg_dev), 1)

    def column(mask, row):
        return jnp.sum(jnp.where(mask, row, 0.0), axis=1, keepdims=True)

    def follow(row, after):
        edge = (sub == seg_dev - 1) & (lane == 0)
        return column(lane == sub + 1, row) + column(edge, after)

    same = lane == sub
    pos = (lax.broadcasted_iota(jnp.int32, (1, rows), 1) + c * rows).astype(F32)
    own_col, own_end = column(same, own_row), follow(own_row, next_row)
    end_row = jnp.full((1, seg_dev), float(rows * n), F32)

    def belongs(first, last):
        return jnp.where((first <= pos) & (pos < last), 1.0, 0.0).astype(BF)

    member[0:seg_dev] = belongs(column(same, prev_row), follow(prev_row, own_row))
    member[seg_dev:2 * seg_dev] = belongs(own_col, own_end)
    member[2 * seg_dev:] = belongs(column(same, next_row), follow(next_row, end_row))

    def near_args(kind):
        return (near_out.at[kind, 0], near_out.at[kind, 1], near_in.at[kind],
                near_send.at[kind], near_recv.at[kind])

    for kind, load, rows_ref in ((0, cot_load, cot), (1, tok_load, tok)):
        load.wait()
        near_out[kind, 0] = mm(member[2 * seg_dev:], rows_ref[...]).astype(BF)
        near_out[kind, 1] = mm(member[0:seg_dev], rows_ref[...]).astype(BF)
        near_start(*near_args(kind))
    for o in range(1, dp):
        for i in range(3):
            w_copy(o, i).start()
    sum_cot = mm(member[seg_dev:2 * seg_dev], cot[...])
    sum_tok = mm(member[seg_dev:2 * seg_dev], tok[...])
    for kind in range(2):
        near_clear(near_in.at[kind])

    near_wait(*near_args(0))
    grad_sum = sum_cot + near_in[0, 0].astype(F32) + near_in[0, 1].astype(F32)
    head_out[...] = grad_sum[0:8]

    def head_copy():
        return remote(head_out, head_in, head_send.at[0], head_recv.at[0], ctx=c - 1)

    @pl.when(has_prev)
    def _():
        head_copy().start()

    near_wait(*near_args(1))
    count = own_end - own_col
    pooled = (sum_tok + near_in[1, 0].astype(F32) + near_in[1, 1].astype(F32)) / count
    rms = jnp.sqrt(jnp.mean(pooled * pooled, axis=-1, keepdims=True) + 1e-06)
    normed = pooled / rms

    def spot(where):
        return gath.at[pl.ds(pl.multiple_of(where * seg_dev, seg_dev), seg_dev)]

    def hop(src_chip, sems, **where):
        at = 2 * src_chip + core
        return remote(spot(at), spot(at), sems.at[src_chip], gath_recv.at[at], **where)

    def go_right(src):
        return hop(src, right_send, ctx=c + 2)

    def go_left(src):
        return hop(src, left_send, ctx=c - 2)

    def go_pair(src):
        return hop(src, pair_send, ctx=mate)

    def arrival(where):
        return remote(spot(where), spot(where), right_send.at[0], gath_recv.at[where], ctx=mate)

    not_last, not_first = chip < chips - 1, chip > 0
    own_at = pl.ds(pl.multiple_of(c * seg_dev, seg_dev), seg_dev)
    gath[own_at] = (normed * gain[...]).astype(BF)

    @pl.when(not_last)
    def _():
        go_right(chip).start()

    @pl.when(not_first)
    def _():
        go_left(chip).start()

    go_pair(chip).start()

    def relay(s):
        @pl.when(chip - s >= 0)
        def _():
            arrival(c - 2 * s).wait_recv()

            @pl.when(not_last)
            def _():
                go_right(chip - s).start()

            go_pair(chip - s).start()

        @pl.when(chip + s < chips)
        def _():
            arrival(c + 2 * s).wait_recv()

            @pl.when(not_first)
            def _():
                go_left(chip + s).start()

            go_pair(chip + s).start()

    def datt_copy(o):
        to = lax.rem(c + o, n)
        cols = pl.ds(pl.multiple_of(lax.rem(to, heads) * HEAD, HEAD), HEAD)
        return remote(grads.at[:, cols], datt.at[own_at], datt_send.at[o - 1], datt_recv.at[o - 1],
                      ctx=to)

    def datt_arrival(o):
        src = lax.rem(c + n - o, n)
        at = pl.ds(pl.multiple_of(src * seg_dev, seg_dev), seg_dev)
        return remote(grads.at[:, head_at], datt.at[at], datt_send.at[o - 1], datt_recv.at[o - 1],
                      ctx=mate)

    def forward_wo():
        for o in range(1, dp):
            wo_arrival(o, core, wo_send, wo_recv).wait_recv()
            wo_arrival(o, core, wo_fsend, wo_frecv).start()

    def own_datt():
        own_loads[3].wait()
        for o in range(1, dp):
            wo_arrival(o, 1 - core, wo_fsend, wo_frecv).wait_recv()
        grads[...] = mm_nt(grad_sum.astype(BF), wout[...]).astype(BF)
        for o in range(1, n):
            datt_copy(o).start()
        datt[own_at] = grads[:, head_at]

    for s in range(1, chips):
        relay(s)
        if s == 1:
            forward_wo()
        if s == min(2, chips - 1):
            own_datt()

    for o in range(1, dp):
        for i in range(3):
            w_arrival(o, i).wait_recv()
    for load in own_loads[:3]:
        load.wait()
    for other in range(chips):
        arrival(2 * other + 1 - core).wait_recv()

    step = 512 if segs % 512 == 0 else seg_dev

    def project(b, _):
        at = pl.ds(pl.multiple_of(b * step, step), step)
        qkv[at] = mm(gath[at], wcat[...]).astype(BF)
        return 0

    lax.fori_loop(0, segs // step, project, 0)
    for o in range(1, n):
        datt_arrival(o).wait_recv()
    shifted = pltpu.roll(datt[...].astype(F32), segs - 1, 0)
    last = lax.broadcasted_iota(jnp.int32, (segs, HEAD), 0) == segs - 1
    datt[...] = jnp.where(last, 0.0, shifted).astype(BF)

    dkv[...] = jnp.zeros_like(dkv)
    if parts > 1:
        dqkv[...] = jnp.zeros_like(dqkv)
    block = 2 * seg_dev

    def attend(q_at, first, klen):
        q = qkv[q_at, 0:HEAD]
        key = qkv[0:klen, HEAD:2 * HEAD]
        value = qkv[0:klen, 2 * HEAD:]
        grad = datt[q_at]
        score = mm_nt(q, key) * scale
        allowed = (lax.broadcasted_iota(jnp.int32, (block, klen), 1)
                   <= lax.broadcasted_iota(jnp.int32, (block, klen), 0) + first)
        score = jnp.where(allowed, score, -1e30)
        peak = jnp.max(score, axis=-1, keepdims=True)
        expo = jnp.where(allowed, jnp.exp(score - peak), 0.0)
        probs = expo / jnp.sum(expo, axis=-1, keepdims=True)
        probs_b = probs.astype(BF)
        attended = mm(probs_b, value).astype(BF).astype(F32)
        delta = jnp.sum(grad.astype(F32) * attended, axis=-1, keepdims=True)
        dscore = (probs * (mm_nt(grad, value) - delta)).astype(BF)
        dqkv[q_at, 0:HEAD] = (mm(dscore, key) * scale).astype(BF)
        dkv[0:klen, 0:HEAD] += mm_tn(dscore, q)
        dkv[0:klen, HEAD:] += mm_tn(probs_b, grad)

    if parts > 1:
        per = segs // parts // block

        def body(b, _):
            first = pl.multiple_of((r * per + b) * block, block)
            attend(pl.ds(first, block), first, segs)
            return 0

        lax.fori_loop(0, per, body, 0)

    def sib_copy(t):
        return remote(part.at[1 - core, t], sib.at[t], sib_send.at[t], sib_recv.at[t], ctx=mate)

    def rs_copy(t):
        return remote(red.at[t], rs.at[chip], rs_send.at[t], rs_recv.at[chip], ctx=2 * t + core)

    def rs_arrival(t):
        return remote(red.at[t], rs.at[t], rs_send.at[t], rs_recv.at[t], ctx=mate)

    def term(t):
        at = slice(t * block, (t + 1) * block)
        dqkv[at, HEAD:2 * HEAD] = (dkv[at, 0:HEAD] * scale).astype(BF)
        dqkv[at, 2 * HEAD:] = dkv[at, HEAD:].astype(BF)
        both = mm_nt(dqkv[at], wcat[...])
        part[0, t] = both[0:seg_dev].astype(BF)
        part[1, t] = both[seg_dev:].astype(BF)
        sib_copy(t).start()

    def push(t):
        sib_copy(t).wait_recv()
        red[t] = (part[core, t].astype(F32) + sib[t].astype(F32)).astype(BF)

        @pl.when(chip != t)
        def _():
            rs_copy(t).start()

    for t in reversed(range(chips)):
        if parts == 1:
            attend(slice(t * block, (t + 1) * block), t * block, (t + 1) * block)
        term(t)
        if t + 1 < chips:
            push(t + 1)
    push(0)

    for other in range(chips):
        @pl.when(not_last & (other <= chip))
        def _():
            go_right(other).wait_send()

        @pl.when(not_first & (other >= chip))
        def _():
            go_left(other).wait_send()

        go_pair(other).wait_send()
        sib_copy(other).wait_send()
    for o in range(1, dp):
        for i in range(3):
            w_copy(o, i).wait_send()
        wo_copy(o).wait_send()
        wo_arrival(o, core, wo_fsend, wo_frecv).wait_send()
    for o in range(1, n):
        datt_copy(o).wait_send()

    @pl.when(has_prev)
    def _():
        head_copy().wait_send()

    @pl.when(has_next)
    def _():
        head_copy().wait_recv()

    @pl.when(jnp.logical_not(has_next))
    def _():
        head_in[...] = jnp.zeros_like(head_in)

    near_clear(seg_in)
    rolled = pltpu.roll(grad_sum, seg_dev - 1, 0)
    ends = lax.broadcasted_iota(jnp.int32, (seg_dev, width), 0) == seg_dev - 1
    dout = jnp.where(ends, head_in[0:1], rolled)

    dnormin = red[chip].astype(F32)
    for o in range(1, chips):
        t = lax.rem(chip + o, chips)
        rs_arrival(t).wait_recv()
        dnormin = dnormin + rs[t].astype(F32)

    scaled = dnormin * gain[...]
    dpooled = dout + (scaled - normed * jnp.mean(scaled * normed, axis=-1, keepdims=True)) / rms
    seg_out[...] = (dpooled / count).astype(BF)
    near_start(seg_out, seg_out, seg_in, seg_send, seg_recv)
    window[seg_dev:2 * seg_dev] = seg_out[...]
    for t in range(chips):
        @pl.when(chip != t)
        def _():
            rs_copy(t).wait_send()
    near_wait(seg_out, seg_out, seg_in, seg_send, seg_recv)
    window[0:seg_dev] = seg_in[0]
    window[2 * seg_dev:] = seg_in[1]


def per_device(tokens, starts, gain, w_query, w_key, w_value, w_out, cotangent):
    n, dp = lax.axis_size("ctx"), lax.axis_size("dp")
    chips = n // 2
    rows, width = tokens.shape[1:]
    seg_dev = starts.shape[1]
    segs = n * seg_dev
    dma = pltpu.SemaphoreType.DMA
    vmem = pltpu.VMEM
    scratch = [
        vmem((rows, width), BF), vmem((rows, width), BF),
        vmem((8, 128), jnp.int32), vmem((2, 8, 128), jnp.int32),
        vmem((2, 2, seg_dev, width), BF), vmem((2, 2, seg_dev, width), BF),
        vmem((8, width), F32), vmem((8, width), F32),
        vmem((segs, width), BF),
        vmem((width, 3 * HEAD), BF),
        vmem((dp * w_out.shape[0], width), BF),
        vmem((seg_dev, dp * w_out.shape[0]), BF),
        vmem((segs, HEAD), BF),
        vmem((segs, 3 * HEAD), BF),
        vmem((segs, 3 * HEAD), BF),
        vmem((segs, 2 * HEAD), F32),
        vmem((2, chips, seg_dev, width), BF),
        vmem((chips, seg_dev, width), BF),
        vmem((chips, seg_dev, width), BF),
        vmem((chips, seg_dev, width), BF),
        vmem((seg_dev, width), BF),
        vmem((2, seg_dev, width), BF),
        dma((2,)), dma((2,)), dma((2,)), dma((2, 2)), dma((2, 2)), dma((1,)), dma((1,)), dma((2,)), dma((2,)),
        dma((dp - 1, 3)), dma((dp - 1, 3)), dma((3,)),
        dma((dp - 1,)), dma((dp - 1,)), dma((1,)), dma((dp - 1,)), dma((dp - 1,)),
        dma((chips,)), dma((chips,)), dma((chips,)), dma((n,)), dma((n - 1,)), dma((n - 1,)),
        dma((chips,)), dma((chips,)), dma((chips,)), dma((chips,)),
    ]
    here, there = pl.BlockSpec(memory_space=pltpu.VMEM), pl.BlockSpec(memory_space=pl.ANY)
    window, member = pl.pallas_call(
        functools.partial(kernel, n, dp),
        out_shape=(
            jax.ShapeDtypeStruct((3 * seg_dev, width), BF),
            jax.ShapeDtypeStruct((3 * seg_dev, rows), BF),
        ),
        in_specs=[there, here, here, there, there, there, there, there],
        out_specs=(here, here),
        scratch_shapes=scratch,
        compiler_params=pltpu.CompilerParams(
            collective_id=0, has_side_effects=True, vmem_limit_bytes=56 * 1024 * 1024
        ),
    )(tokens, starts, gain[None], w_query, w_key, w_value, w_out, cotangent)
    return (cotangent[0].astype(F32) + mm_tn(member, window)).astype(BF)[None]


def solution(mesh):
    return jax.shard_map(
        per_device,
        mesh=mesh,
        in_specs=(
            P("dp", "ctx", None),
            P("dp", "ctx"),
            P(),
            P("dp", None),
            P("dp", None),
            P("dp", None),
            P("dp", None),
            P("dp", "ctx", None),
        ),
        out_specs=P("dp", "ctx", None),
        check_vma=False,
    )
```

time: 58.9 us -> 52.8 us (0.90)
  the two profiles are of different devices: /device:TPU:17 before, /device:TPU:1 now
where the time goes in v2:
time: 52.8 us; the launch traced here: 52.6 us
  Pallas kernels  50 us (95%)
  matrix products  2.55 us (5%)
    pallas_call x1, Pallas kernels, per_device(): pl.pallas_call(functools.partial(kernel, n, dp), out_shape=(jax.ShapeDtyp...  50 us
    dot_general x1, matrix products, dot(): lax.dot_general(left, right, ((dims[0], dims[1]), ((), ())), preferred_el...  2.55 us

profile of v2, /device:TPU:1, one launch (start us, length us, event | category | flops | bytes accessed | tf_op | source)
XLA Modules:
  0.0 52.6 jit_solution(14033445460398225430)
XLA Ops:
  0.0 0.0 copy-start
  0.0 50.0 %shard_map.82 = (bf16[192,1024]{1,0:T(8,128)(2,1)}, bf16[192,512]{1,0:T(8,128)(2,1)}) custom-call(bf16[1,512,1024]{2,1,0:T(8,128)(2,1)} %tok_hbm.1, s32[1,64]{1,0:T(1,128)} %starts.1, f32[1,1024]{1,0:T(1,128)} %bitcast.8, bf16[256,1024]{1,0:T(8,128)(2,1)} %wq.1, bf16[256,1024]{1,0:T(8,128)(2,1)} %wk.1, bf16[256,1024]{1,0:T(8,128)(2,1)} %wv.1, ...), custom_call_target="tpu_custom_call" | custom-call | tf_op jit(solution)/shard_map/pallas_call | solution.py:482
  50.0 0.0 copy-done
  50.0 2.5 %fusion.1 = bf16[1,512,1024]{2,1,0:T(8,128)(2,1)} fusion(bf16[192,512]{1,0:T(8,128)(2,1)} %get-tuple-element.7, bf16[192,1024]{1,0:T(8,128)(2,1)} %get-tuple-element.8, bf16[1,512,1024]{2,1,0:T(8,128)(2,1)S(1)} %copy-done), kind=kOutput, calls=%fused_computation.2 | convolution fusion | flops 202899456 | bytes 2686976 | tf_op jit(solution)/shard_map/dot_general | solution.py:17
Async XLA Ops:
  0.0 50.0 %copy-start = (bf16[1,512,1024]{2,1,0:T(8,128)(2,1)S(1)}, bf16[1,512,1024]{2,1,0:T(8,128)(2,1)}, u32[]{:S(2)}) copy-start(bf16[1,512,1024]{2,1,0:T(8,128)(2,1)} %cot_hbm.1) | copy-start | bytes 3145732

commit v3 on v2

--- a/solution.py
+++ b/solution.py
@@ -38,9 +38,9 @@
 
 def kernel(
     n, dp,
-    tok_hbm, starts, gain, wq, wk, wv, wo, cot_hbm, window, member,
-    tok, cot, st_mine, st_near, near_out, near_in, head_out, head_in, gath, wcat, wout, grads, datt,
-    qkv, dqkv, dkv, part, sib, red, rs, seg_out, seg_in,
+    tok_hbm, starts, gain, wq, wk, wv, wo, cot_hbm, window, spread_at,
+    member, tok, cot, st_mine, st_near, near_out, near_in, head_out, head_in, gath, wcat, wout, grads, datt,
+    qkv, dqkv, dkv, prob_s, dscore_s, part, sib, red, rs, seg_out, seg_in,
     in_sem, st_send, st_recv, near_send, near_recv, head_send, head_recv, seg_send, seg_recv,
     w_send, w_recv, w_local, wo_send, wo_recv, wo_local, wo_fsend, wo_frecv,
     right_send, left_send, pair_send, gath_recv, datt_send, datt_recv,
@@ -186,13 +186,22 @@
         near_out[kind, 0] = mm(member[2 * seg_dev:], rows_ref[...]).astype(BF)
         near_out[kind, 1] = mm(member[0:seg_dev], rows_ref[...]).astype(BF)
         near_start(*near_args(kind))
-    for o in range(1, dp):
-        for i in range(3):
-            w_copy(o, i).start()
     sum_cot = mm(member[seg_dev:2 * seg_dev], cot[...])
     sum_tok = mm(member[seg_dev:2 * seg_dev], tok[...])
     for kind in range(2):
         near_clear(near_in.at[kind])
+
+    def across(col):
+        return jnp.sum(jnp.where(same, col, 0.0), axis=0, keepdims=True)
+
+    pos_col = (lax.broadcasted_iota(jnp.int32, (rows, 1), 0) + c * rows).astype(F32)
+    for k, (first, last) in enumerate((
+        (prev_row, across(follow(prev_row, own_row))),
+        (own_row, across(own_end)),
+        (next_row, across(follow(next_row, end_row))),
+    )):
+        inside = (first <= pos_col) & (pos_col < last)
+        spread_at[:, k * seg_dev:(k + 1) * seg_dev] = jnp.where(inside, 1.0, 0.0).astype(BF)
 
     near_wait(*near_args(0))
     grad_sum = sum_cot + near_in[0, 0].astype(F32) + near_in[0, 1].astype(F32)
@@ -243,6 +252,9 @@
         go_left(chip).start()
 
     go_pair(chip).start()
+    for o in range(1, dp):
+        for i in range(3):
+            w_copy(o, i).start()
 
     def relay(s):
         @pl.when(chip - s >= 0)
@@ -320,8 +332,8 @@
     last = lax.broadcasted_iota(jnp.int32, (segs, HEAD), 0) == segs - 1
     datt[...] = jnp.where(last, 0.0, shifted).astype(BF)
 
-    dkv[...] = jnp.zeros_like(dkv)
     if parts > 1:
+        dkv[...] = jnp.zeros_like(dkv)
         dqkv[...] = jnp.zeros_like(dqkv)
     block = 2 * seg_dev
 
@@ -342,18 +354,25 @@
         delta = jnp.sum(grad.astype(F32) * attended, axis=-1, keepdims=True)
         dscore = (probs * (mm_nt(grad, value) - delta)).astype(BF)
         dqkv[q_at, 0:HEAD] = (mm(dscore, key) * scale).astype(BF)
-        dkv[0:klen, 0:HEAD] += mm_tn(dscore, q)
-        dkv[0:klen, HEAD:] += mm_tn(probs_b, grad)
+        return q, grad, probs_b, dscore
 
     if parts > 1:
         per = segs // parts // block
 
         def body(b, _):
             first = pl.multiple_of((r * per + b) * block, block)
-            attend(pl.ds(first, block), first, segs)
+            q, grad, probs_b, dscore = attend(pl.ds(first, block), first, segs)
+            dkv[:, 0:HEAD] += mm_tn(dscore, q)
+            dkv[:, HEAD:] += mm_tn(probs_b, grad)
             return 0
 
         lax.fori_loop(0, per, body, 0)
+    else:
+        for t in range(chips):
+            at, upto = slice(t * block, (t + 1) * block), (t + 1) * block
+            _, _, probs_b, dscore = attend(at, t * block, upto)
+            prob_s[at, 0:upto] = probs_b
+            dscore_s[at, 0:upto] = dscore
 
     def sib_copy(t):
         return remote(part.at[1 - core, t], sib.at[t], sib_send.at[t], sib_recv.at[t], ctx=mate)
@@ -366,8 +385,13 @@
 
     def term(t):
         at = slice(t * block, (t + 1) * block)
-        dqkv[at, HEAD:2 * HEAD] = (dkv[at, 0:HEAD] * scale).astype(BF)
-        dqkv[at, 2 * HEAD:] = dkv[at, HEAD:].astype(BF)
+        if parts > 1:
+            dkey, dvalue = dkv[at, 0:HEAD], dkv[at, HEAD:]
+        else:
+            dkey = mm_tn(dscore_s[t * block:, at], qkv[t * block:, 0:HEAD])
+            dvalue = mm_tn(prob_s[t * block:, at], datt[t * block:])
+        dqkv[at, HEAD:2 * HEAD] = (dkey * scale).astype(BF)
+        dqkv[at, 2 * HEAD:] = dvalue.astype(BF)
         both = mm_nt(dqkv[at], wcat[...])
         part[0, t] = both[0:seg_dev].astype(BF)
         part[1, t] = both[seg_dev:].astype(BF)
@@ -381,13 +405,12 @@
         def _():
             rs_copy(t).start()
 
-    for t in reversed(range(chips)):
-        if parts == 1:
-            attend(slice(t * block, (t + 1) * block), t * block, (t + 1) * block)
+    order = [t // 2 if t % 2 == 0 else chips - 1 - t // 2 for t in range(chips)]
+    for at, t in enumerate(order):
         term(t)
-        if t + 1 < chips:
-            push(t + 1)
-    push(0)
+        if at > 0:
+            push(order[at - 1])
+    push(order[-1])
 
     for other in range(chips):
         @pl.when(not_last & (other <= chip))
@@ -453,7 +476,10 @@
     segs = n * seg_dev
     dma = pltpu.SemaphoreType.DMA
     vmem = pltpu.VMEM
+    heads = w_query.shape[1] // HEAD
+    whole = n == heads
     scratch = [
+        vmem((3 * seg_dev, rows), BF),
         vmem((rows, width), BF), vmem((rows, width), BF),
         vmem((8, 128), jnp.int32), vmem((2, 8, 128), jnp.int32),
         vmem((2, 2, seg_dev, width), BF), vmem((2, 2, seg_dev, width), BF),
@@ -465,7 +491,9 @@
         vmem((segs, HEAD), BF),
         vmem((segs, 3 * HEAD), BF),
         vmem((segs, 3 * HEAD), BF),
-        vmem((segs, 2 * HEAD), F32),
+        vmem((8, 2 * HEAD) if whole else (segs, 2 * HEAD), F32),
+        vmem((segs, segs) if whole else (16, HEAD), BF),
+        vmem((segs, segs) if whole else (16, HEAD), BF),
         vmem((2, chips, seg_dev, width), BF),
         vmem((chips, seg_dev, width), BF),
         vmem((chips, seg_dev, width), BF),
@@ -479,11 +507,11 @@
         dma((chips,)), dma((chips,)), dma((chips,)), dma((chips,)),
     ]
     here, there = pl.BlockSpec(memory_space=pltpu.VMEM), pl.BlockSpec(memory_space=pl.ANY)
-    window, member = pl.pallas_call(
+    window, spread_at = pl.pallas_call(
         functools.partial(kernel, n, dp),
         out_shape=(
             jax.ShapeDtypeStruct((3 * seg_dev, width), BF),
-            jax.ShapeDtypeStruct((3 * seg_dev, rows), BF),
+            jax.ShapeDtypeStruct((rows, 3 * seg_dev), BF),
         ),
         in_specs=[there, here, here, there, there, there, there, there],
         out_specs=(here, here),
@@ -492,7 +520,7 @@
             collective_id=0, has_side_effects=True, vmem_limit_bytes=56 * 1024 * 1024
         ),
     )(tokens, starts, gain[None], w_query, w_key, w_value, w_out, cotangent)
-    return (cotangent[0].astype(F32) + mm_tn(member, window)).astype(BF)[None]
+    return (cotangent[0].astype(F32) + mm(spread_at, window)).astype(BF)[None]
 
 
 def solution(mesh):

time: 52.8 us -> 53.8 us (1.019)
  Pallas kernels: 50 us -> 51.1 us
    pallas_call x1, Pallas kernels: 50 us -> 51.1 us  [per_device(): pl.pallas_call(functools.partial(kernel, n, dp), out_shape=(jax.ShapeDtyp...]
where the time goes in v3:
time: 53.8 us; the launch traced here: 53.6 us
  Pallas kernels  51.1 us (95%)
  matrix products  2.48 us (5%)
    pallas_call x1, Pallas kernels, per_device(): pl.pallas_call(functools.partial(kernel, n, dp), out_shape=(jax.ShapeDtyp...  51.1 us
    dot_general x1, matrix products, dot(): lax.dot_general(left, right, ((dims[0], dims[1]), ((), ())), preferred_el...  2.48 us

profile of v3, /device:TPU:1, one launch (start us, length us, event | category | flops | bytes accessed | tf_op | source)
XLA Modules:
  0.0 53.6 jit_solution(11229219315948241953)
XLA Ops:
  0.0 0.0 copy-start
  0.0 51.1 %shard_map.82 = (bf16[192,1024]{1,0:T(8,128)(2,1)}, bf16[512,192]{1,0:T(8,128)(2,1)}) custom-call(bf16[1,512,1024]{2,1,0:T(8,128)(2,1)} %tok_hbm.1, s32[1,64]{1,0:T(1,128)} %starts.1, f32[1,1024]{1,0:T(1,128)} %bitcast.8, bf16[256,1024]{1,0:T(8,128)(2,1)} %wq.1, bf16[256,1024]{1,0:T(8,128)(2,1)} %wk.1, bf16[256,1024]{1,0:T(8,128)(2,1)} %wv.1, ...), custom_call_target="tpu_custom_call" | custom-call | tf_op jit(solution)/shard_map/pallas_call | solution.py:510
  51.1 0.0 copy-done
  51.1 2.5 %fusion.1 = bf16[1,512,1024]{2,1,0:T(8,128)(2,1)} fusion(bf16[512,192]{1,0:T(8,128)(2,1)} %get-tuple-element.7, bf16[192,1024]{1,0:T(8,128)(2,1)} %get-tuple-element.8, bf16[1,512,1024]{2,1,0:T(8,128)(2,1)S(1)} %copy-done), kind=kOutput, calls=%fused_computation.2 | convolution fusion | flops 202899456 | bytes 2686976 | tf_op jit(solution)/shard_map/dot_general | solution.py:17
Async XLA Ops:
  0.0 51.1 %copy-start = (bf16[1,512,1024]{2,1,0:T(8,128)(2,1)S(1)}, bf16[1,512,1024]{2,1,0:T(8,128)(2,1)}, u32[]{:S(2)}) copy-start(bf16[1,512,1024]{2,1,0:T(8,128)(2,1)} %cot_hbm.1) | copy-start | bytes 3145732

commit v4 on v3

--- a/solution.py
+++ b/solution.py
@@ -377,11 +377,21 @@
     def sib_copy(t):
         return remote(part.at[1 - core, t], sib.at[t], sib_send.at[t], sib_recv.at[t], ctx=mate)
 
-    def rs_copy(t):
-        return remote(red.at[t], rs.at[chip], rs_send.at[t], rs_recv.at[chip], ctx=2 * t + core)
-
-    def rs_arrival(t):
-        return remote(red.at[t], rs.at[t], rs_send.at[t], rs_recv.at[t], ctx=mate)
+    def piece(k):
+        return pl.ds(k * (seg_dev // 2), seg_dev // 2)
+
+    def way(leftward):
+        side = jnp.where(leftward, 0, 1)
+        return side, c + 4 * side - 2
+
+    def rs_copy(t, k, leftward):
+        side, to = way(leftward)
+        return remote(red.at[t, piece(k)], rs.at[side, t, piece(k)],
+                      rs_send.at[t, k], rs_recv.at[side, t, k], ctx=to)
+
+    def rs_arrival(t, k, side):
+        return remote(red.at[t, piece(k)], rs.at[side, t, piece(k)],
+                      rs_send.at[t, k], rs_recv.at[side, t, k], ctx=mate)
 
     def term(t):
         at = slice(t * block, (t + 1) * block)
@@ -401,9 +411,16 @@
         sib_copy(t).wait_recv()
         red[t] = (part[core, t].astype(F32) + sib[t].astype(F32)).astype(BF)
 
-        @pl.when(chip != t)
-        def _():
-            rs_copy(t).start()
+        if t > 0:
+            @pl.when(chip == 0)
+            def _():
+                for k in range(2):
+                    rs_copy(t, k, False).start()
+        if t < chips - 1:
+            @pl.when(chip == chips - 1)
+            def _():
+                for k in range(2):
+                    rs_copy(t, k, True).start()
 
     order = [t // 2 if t % 2 == 0 else chips - 1 - t // 2 for t in range(chips)]
     for at, t in enumerate(order):
@@ -411,6 +428,25 @@
         if at > 0:
             push(order[at - 1])
     push(order[-1])
+
+    def pass_on(i, leftward):
+        t = jnp.where(leftward, i, chips - 1 - i)
+        inner_chip = (chip > 0) & (chip < chips - 1)
+        passes = jnp.where(leftward, chip - t, t - chip) > 0
+
+        @pl.when(inner_chip & passes)
+        def _():
+            side, _ = way(leftward)
+            for k in range(2):
+                rs_arrival(t, k, side).wait_recv()
+                at = piece(k)
+                red[t, at] = (red[t, at].astype(F32) + rs[side, t, at].astype(F32)).astype(BF)
+                rs_copy(t, k, leftward).start()
+
+    left_first = 2 * chip >= chips
+    for i in range(chips - 1):
+        pass_on(i, left_first)
+        pass_on(i, jnp.logical_not(left_first))
 
     for other in range(chips):
         @pl.when(not_last & (other <= chip))
@@ -448,11 +484,24 @@
     ends = lax.broadcasted_iota(jnp.int32, (seg_dev, width), 0) == seg_dev - 1
     dout = jnp.where(ends, head_in[0:1], rolled)
 
-    dnormin = red[chip].astype(F32)
-    for o in range(1, chips):
-        t = lax.rem(chip + o, chips)
-        rs_arrival(t).wait_recv()
-        dnormin = dnormin + rs[t].astype(F32)
+    @pl.when(chip == chips - 1)
+    def _():
+        rs[0, chips - 1] = jnp.zeros_like(rs[0, chips - 1])
+
+    @pl.when(chip == 0)
+    def _():
+        rs[1, 0] = jnp.zeros_like(rs[1, 0])
+
+    for k in range(2):
+        @pl.when(not_first)
+        def _():
+            rs_arrival(chip, k, 1).wait_recv()
+
+        @pl.when(not_last)
+        def _():
+            rs_arrival(chip, k, 0).wait_recv()
+
+    dnormin = red[chip].astype(F32) + rs[0, chip].astype(F32) + rs[1, chip].astype(F32)
 
     scaled = dnormin * gain[...]
     dpooled = dout + (scaled - normed * jnp.mean(scaled * normed, axis=-1, keepdims=True)) / rms
@@ -462,10 +511,15 @@
     for t in range(chips):
         @pl.when(chip != t)
         def _():
-            rs_copy(t).wait_send()
+            for k in range(2):
+                rs_arrival(t, k, 0).wait_send()
     near_wait(seg_out, seg_out, seg_in, seg_send, seg_recv)
     window[0:seg_dev] = seg_in[0]
     window[2 * seg_dev:] = seg_in[1]
+
+
+def spread_kernel(spread_at, window, cot, out):
+    out[0] = (cot[0].astype(F32) + mm(spread_at[...], window[...])).astype(BF)
 
 
 def per_device(tokens, starts, gain, w_query, w_key, w_value, w_out, cotangent):
@@ -497,14 +551,14 @@
         vmem((2, chips, seg_dev, width), BF),
         vmem((chips, seg_dev, width), BF),
         vmem((chips, seg_dev, width), BF),
-        vmem((chips, seg_dev, width), BF),
+        vmem((2, chips, seg_dev, width), BF),
         vmem((seg_dev, width), BF),
         vmem((2, seg_dev, width), BF),
         dma((2,)), dma((2,)), dma((2,)), dma((2, 2)), dma((2, 2)), dma((1,)), dma((1,)), dma((2,)), dma((2,)),
         dma((dp - 1, 3)), dma((dp - 1, 3)), dma((3,)),
         dma((dp - 1,)), dma((dp - 1,)), dma((1,)), dma((dp - 1,)), dma((dp - 1,)),
         dma((chips,)), dma((chips,)), dma((chips,)), dma((n,)), dma((n - 1,)), dma((n - 1,)),
-        dma((chips,)), dma((chips,)), dma((chips,)), dma((chips,)),
+        dma((chips,)), dma((chips,)), dma((chips, 2)), dma((2, chips, 2)),
     ]
     here, there = pl.BlockSpec(memory_space=pltpu.VMEM), pl.BlockSpec(memory_space=pl.ANY)
     window, spread_at = pl.pallas_call(
@@ -520,7 +574,19 @@
             collective_id=0, has_side_effects=True, vmem_limit_bytes=56 * 1024 * 1024
         ),
     )(tokens, starts, gain[None], w_query, w_key, w_value, w_out, cotangent)
-    return (cotangent[0].astype(F32) + mm(spread_at, window)).astype(BF)[None]
+    step = 128
+    return pl.pallas_call(
+        spread_kernel,
+        grid=(rows // step,),
+        out_shape=jax.ShapeDtypeStruct(tokens.shape, BF),
+        in_specs=[
+            pl.BlockSpec((step, 3 * seg_dev), lambda i: (i, 0)),
+            pl.BlockSpec((3 * seg_dev, width), lambda i: (0, 0)),
+            pl.BlockSpec((1, step, width), lambda i: (0, i, 0)),
+        ],
+        out_specs=pl.BlockSpec((1, step, width), lambda i: (0, i, 0)),
+        compiler_params=pltpu.CompilerParams(vmem_limit_bytes=16 * 1024 * 1024),
+    )(spread_at, window, cotangent)
 
 
 def solution(mesh):

time: 53.8 us -> 57.5 us (1.069)
  Pallas kernels: 51.1 us -> 54.9 us
  matrix products: 2.48 us -> 0 us
  local copies, waits for them, and re-layouts: 0.01 us -> 1.94 us
    dot_general x1 -> x0, matrix products: 2.48 us -> none  [dot(): lax.dot_general(left, right, ((dims[0], dims[1]), ((), ())), preferred_el...]
    pallas_call x0 -> x1, Pallas kernels: none -> 2.08 us  [per_device(): pl.pallas_call(spread_kernel, grid=(rows // step,), out_shape=jax.ShapeDt...]
    unnamed x2 -> x6, local copies, waits for them, and re-layouts: 0.01 us -> 1.94 us
    pallas_call x1, Pallas kernels: 51.1 us -> 52.8 us  [per_device(): pl.pallas_call(functools.partial(kernel, n, dp), out_shape=(jax.ShapeDtyp...]
where the time goes in v4:
time: 57.5 us; the launch traced here: 56.9 us
  Pallas kernels  54.9 us (95%)
  local copies, waits for them, and re-layouts  1.94 us (3%)
    pallas_call x1, Pallas kernels, per_device(): pl.pallas_call(functools.partial(kernel, n, dp), out_shape=(jax.ShapeDtyp...  52.8 us
    pallas_call x1, Pallas kernels, per_device(): pl.pallas_call(spread_kernel, grid=(rows // step,), out_shape=jax.ShapeDt...  2.08 us
    unnamed x6, local copies, waits for them, and re-layouts  1.94 us

profile of v4, /device:TPU:1, one launch (start us, length us, event | category | flops | bytes accessed | tf_op | source)
XLA Modules:
  0.0 56.9 jit_solution(17408112687145954101)
XLA Ops:
  0.0 0.0 copy-start
  0.0 52.8 %shard_map.82 = (bf16[192,1024]{1,0:T(8,128)(2,1)}, bf16[512,192]{1,0:T(8,128)(2,1)}) custom-call(bf16[1,512,1024]{2,1,0:T(8,128)(2,1)} %tok_hbm.1, s32[1,64]{1,0:T(1,128)} %starts.1, f32[1,1024]{1,0:T(1,128)} %bitcast.1, bf16[256,1024]{1,0:T(8,128)(2,1)} %wq.1, bf16[256,1024]{1,0:T(8,128)(2,1)} %wk.1, bf16[256,1024]{1,0:T(8,128)(2,1)} %wv.1, ...), custom_call_target="tpu_custom_call" | custom-call | tf_op jit(solution)/shard_map/pallas_call | solution.py:564
  52.8 0.0 copy-done
  52.8 0.0 copy-start.1
  52.8 1.0 %copy-done.1 = bf16[192,1024]{1,0:T(8,128)(2,1)S(1)} copy-done((bf16[192,1024]{1,0:T(8,128)(2,1)S(1)}, bf16[192,1024]{1,0:T(8,128)(2,1)}, u32[]{:S(2)}) %copy-start.1) | copy-done | bytes 393240
  53.8 0.0 copy-start.2
  53.8 0.9 %copy-done.2 = bf16[512,192]{1,0:T(8,128)(2,1)S(1)} copy-done((bf16[512,192]{1,0:T(8,128)(2,1)S(1)}, bf16[512,192]{1,0:T(8,128)(2,1)}, u32[]{:S(2)}) %copy-start.2) | copy-done | bytes 196632
  54.8 2.1 %shard_map.83 = bf16[1,512,1024]{2,1,0:T(8,128)(2,1)} custom-call(bf16[512,192]{1,0:T(8,128)(2,1)S(1)} %copy-done.2, bf16[192,1024]{1,0:T(8,128)(2,1)S(1)} %copy-done.1, bf16[1,512,1024]{2,1,0:T(8,128)(2,1)S(1)} %copy-done), custom_call_target="tpu_custom_call" | custom-call | tf_op jit(solution)/shard_map/pallas_call | solution.py:578
Async XLA Ops:
  0.0 52.8 %copy-start = (bf16[1,512,1024]{2,1,0:T(8,128)(2,1)S(1)}, bf16[1,512,1024]{2,1,0:T(8,128)(2,1)}, u32[]{:S(2)}) copy-start(bf16[1,512,1024]{2,1,0:T(8,128)(2,1)} %cot.1) | copy-start | bytes 3145732
  52.8 1.0 %copy-start.1 = (bf16[192,1024]{1,0:T(8,128)(2,1)S(1)}, bf16[192,1024]{1,0:T(8,128)(2,1)}, u32[]{:S(2)}) copy-start(bf16[192,1024]{1,0:T(8,128)(2,1)} %get-tuple-element.8.window) | copy-start | bytes 1179652
  53.8 0.9 %copy-start.2 = (bf16[512,192]{1,0:T(8,128)(2,1)S(1)}, bf16[512,192]{1,0:T(8,128)(2,1)}, u32[]{:S(2)}) copy-start(bf16[512,192]{1,0:T(8,128)(2,1)} %get-tuple-element.7.spread_at) | copy-start | bytes 589828

commit v5 on v2

--- a/solution.py
+++ b/solution.py
@@ -39,10 +39,10 @@
 def kernel(
     n, dp,
     tok_hbm, starts, gain, wq, wk, wv, wo, cot_hbm, window, member,
-    tok, cot, st_mine, st_near, near_out, near_in, head_out, head_in, gath, wcat, wout, grads, datt,
+    tok, cot, st_mine, st_near, near_out, near_in, head_out, head_in, gath, wcat, gsum, grads, datt,
     qkv, dqkv, dkv, part, sib, red, rs, seg_out, seg_in,
     in_sem, st_send, st_recv, near_send, near_recv, head_send, head_recv, seg_send, seg_recv,
-    w_send, w_recv, w_local, wo_send, wo_recv, wo_local, wo_fsend, wo_frecv,
+    w_send, w_recv, w_local, g_send, g_recv,
     right_send, left_send, pair_send, gath_recv, datt_send, datt_recv,
     sib_send, sib_recv, rs_send, rs_recv,
 ):
@@ -56,7 +56,6 @@
     seg_dev = starts.shape[1]
     segs = n * seg_dev
     w_rows, inner = wq.shape
-    half = w_rows // 2
     heads = inner // HEAD
     parts = n // heads
     h = lax.rem(c, heads)
@@ -71,6 +70,14 @@
     for o in range(1, dp):
         pl.semaphore_signal(barrier, inc=1, device_id={"dp": lax.rem(me + o, dp)},
                             device_id_type=pl.DeviceIdType.MESH)
+    per_row = w_rows // HEAD
+    holder = lax.div(h, per_row)
+    lone = jnp.where(holder == me, 1, 0)
+    for o in range(n):
+        @pl.when((holder != me) | (c != o))
+        def _():
+            pl.semaphore_signal(barrier, inc=1, device_id={"dp": holder, "ctx": o},
+                                device_id_type=pl.DeviceIdType.MESH)
 
     def dp_rows(where, extra=0, size=w_rows):
         return pl.ds(pl.multiple_of(where * w_rows + extra, size), size)
@@ -84,14 +91,13 @@
                               w_local.at[i])
         for i in range(3)
     ]
-    own_loads.append(pltpu.make_async_copy(wo, wout.at[dp_rows(me)], wo_local.at[0]))
     cot_load.start()
     tok_load.start()
     for load in own_loads:
         load.start()
     st_mine[...] = jnp.zeros_like(st_mine)
     st_mine[0:1, 0:seg_dev] = starts[...]
-    pl.semaphore_wait(barrier, n - 1 + dp - 1)
+    pl.semaphore_wait(barrier, n - 1 + dp - 1 + n - lone)
 
     def to_next(src, dst, send, recv):
         return remote(src, dst.at[0], send.at[0], recv.at[0], ctx=c + 1)
@@ -129,18 +135,6 @@
             dst[1] = jnp.zeros_like(dst[1])
 
     near_start(st_mine, st_mine, st_near, st_send, st_recv)
-
-    def wo_copy(o):
-        return remote(wo.at[pl.ds(pl.multiple_of(core * half, half), half)],
-                      wout.at[dp_rows(me, core * half, half)],
-                      wo_send.at[o - 1], wo_recv.at[o - 1], dp=lax.rem(me + o, dp))
-
-    def wo_arrival(o, which, sends, recvs):
-        at = dp_rows(lax.rem(me + dp - o, dp), which * half, half)
-        return remote(wout.at[at], wout.at[at], sends.at[o - 1], recvs.at[o - 1], ctx=mate)
-
-    for o in range(1, dp):
-        wo_copy(o).start()
 
     def w_copy(o, i):
         return remote(mats[i].at[:, head_at], wcat.at[dp_rows(me), pl.ds(i * HEAD, HEAD)],
@@ -150,6 +144,10 @@
         src = lax.rem(me + dp - o, dp)
         return remote(mats[i].at[:, head_at], wcat.at[dp_rows(src), pl.ds(i * HEAD, HEAD)],
                       w_send.at[o - 1, i], w_recv.at[o - 1, i], dp=lax.rem(me + o, dp))
+
+    for o in range(1, dp):
+        for i in range(3):
+            w_copy(o, i).start()
 
     near_wait(st_mine, st_mine, st_near, st_send, st_recv)
     own_row = starts[...].astype(F32)
@@ -186,9 +184,6 @@
         near_out[kind, 0] = mm(member[2 * seg_dev:], rows_ref[...]).astype(BF)
         near_out[kind, 1] = mm(member[0:seg_dev], rows_ref[...]).astype(BF)
         near_start(*near_args(kind))
-    for o in range(1, dp):
-        for i in range(3):
-            w_copy(o, i).start()
     sum_cot = mm(member[seg_dev:2 * seg_dev], cot[...])
     sum_tok = mm(member[seg_dev:2 * seg_dev], tok[...])
     for kind in range(2):
@@ -197,6 +192,21 @@
     near_wait(*near_args(0))
     grad_sum = sum_cot + near_in[0, 0].astype(F32) + near_in[0, 1].astype(F32)
     head_out[...] = grad_sum[0:8]
+
+    def g_rows(where):
+        return gsum.at[pl.ds(pl.multiple_of(where * seg_dev, seg_dev), seg_dev)]
+
+    def g_copy(o):
+        return remote(g_rows(me), g_rows(me), g_send.at[o - 1], g_recv.at[o - 1],
+                      dp=lax.rem(me + o, dp))
+
+    def g_arrival(o):
+        at = g_rows(lax.rem(me + dp - o, dp))
+        return remote(at, at, g_send.at[o - 1], g_recv.at[o - 1], ctx=mate)
+
+    gsum[pl.ds(pl.multiple_of(me * seg_dev, seg_dev), seg_dev)] = grad_sum.astype(BF)
+    for o in range(1, dp):
+        g_copy(o).start()
 
     def head_copy():
         return remote(head_out, head_in, head_send.at[0], head_recv.at[0], ctx=c - 1)
@@ -265,43 +275,45 @@
 
             go_pair(chip + s).start()
 
-    def datt_copy(o):
-        to = lax.rem(c + o, n)
-        cols = pl.ds(pl.multiple_of(lax.rem(to, heads) * HEAD, HEAD), HEAD)
-        return remote(grads.at[:, cols], datt.at[own_at], datt_send.at[o - 1], datt_recv.at[o - 1],
-                      ctx=to)
-
-    def datt_arrival(o):
-        src = lax.rem(c + n - o, n)
+    targets = [(b, j, q) for b in range(dp) for j in range(per_row) for q in range(parts)]
+
+    def datt_copy(at):
+        b, j, q = targets[at]
+        to = me * per_row + j + q * heads
+        return (b != me) | (to != c), remote(
+            grads.at[pl.ds(b * seg_dev, seg_dev), pl.ds(j * HEAD, HEAD)], datt.at[own_at],
+            datt_send.at[at], datt_recv.at[c], dp=b, ctx=to)
+
+    def datt_arrival(src):
         at = pl.ds(pl.multiple_of(src * seg_dev, seg_dev), seg_dev)
-        return remote(grads.at[:, head_at], datt.at[at], datt_send.at[o - 1], datt_recv.at[o - 1],
-                      ctx=mate)
-
-    def forward_wo():
+        return (holder != me) | (src != c), remote(
+            grads.at[pl.ds(0, seg_dev), pl.ds(0, HEAD)], datt.at[at],
+            datt_send.at[src], datt_recv.at[src], ctx=mate)
+
+    def own_datt():
         for o in range(1, dp):
-            wo_arrival(o, core, wo_send, wo_recv).wait_recv()
-            wo_arrival(o, core, wo_fsend, wo_frecv).start()
-
-    def own_datt():
-        own_loads[3].wait()
-        for o in range(1, dp):
-            wo_arrival(o, 1 - core, wo_fsend, wo_frecv).wait_recv()
-        grads[...] = mm_nt(grad_sum.astype(BF), wout[...]).astype(BF)
-        for o in range(1, n):
-            datt_copy(o).start()
-        datt[own_at] = grads[:, head_at]
+            g_arrival(o).wait_recv()
+        grads[...] = mm_nt(gsum[...], wo[...]).astype(BF)
+        for at, (b, j, _) in enumerate(targets):
+            away, copy = datt_copy(at)
+
+            @pl.when(away)
+            def _():
+                copy.start()
+
+            @pl.when(jnp.logical_not(away))
+            def _():
+                datt[own_at] = grads[b * seg_dev:(b + 1) * seg_dev, j * HEAD:(j + 1) * HEAD]
 
     for s in range(1, chips):
         relay(s)
-        if s == 1:
-            forward_wo()
         if s == min(2, chips - 1):
             own_datt()
 
     for o in range(1, dp):
         for i in range(3):
             w_arrival(o, i).wait_recv()
-    for load in own_loads[:3]:
+    for load in own_loads:
         load.wait()
     for other in range(chips):
         arrival(2 * other + 1 - core).wait_recv()
@@ -314,8 +326,13 @@
         return 0
 
     lax.fori_loop(0, segs // step, project, 0)
-    for o in range(1, n):
-        datt_arrival(o).wait_recv()
+    for src in range(n):
+        away, copy = datt_arrival(src)
+
+        @pl.when(away)
+        def _():
+            copy.wait_recv()
+
     shifted = pltpu.roll(datt[...].astype(F32), segs - 1, 0)
     last = lax.broadcasted_iota(jnp.int32, (segs, HEAD), 0) == segs - 1
     datt[...] = jnp.where(last, 0.0, shifted).astype(BF)
@@ -403,10 +420,13 @@
     for o in range(1, dp):
         for i in range(3):
             w_copy(o, i).wait_send()
-        wo_copy(o).wait_send()
-        wo_arrival(o, core, wo_fsend, wo_frecv).wait_send()
-    for o in range(1, n):
-        datt_copy(o).wait_send()
+        g_copy(o).wait_send()
+    for at in range(len(targets)):
+        away, copy = datt_copy(at)
+
+        @pl.when(away)
+        def _():
+            copy.wait_send()
 
     @pl.when(has_prev)
     def _():
@@ -460,8 +480,8 @@
         vmem((8, width), F32), vmem((8, width), F32),
         vmem((segs, width), BF),
         vmem((width, 3 * HEAD), BF),
-        vmem((dp * w_out.shape[0], width), BF),
-        vmem((seg_dev, dp * w_out.shape[0]), BF),
+        vmem((dp * seg_dev, width), BF),
+        vmem((dp * seg_dev, w_out.shape[0]), BF),
         vmem((segs, HEAD), BF),
         vmem((segs, 3 * HEAD), BF),
         vmem((segs, 3 * HEAD), BF),
@@ -474,8 +494,8 @@
         vmem((2, seg_dev, width), BF),
         dma((2,)), dma((2,)), dma((2,)), dma((2, 2)), dma((2, 2)), dma((1,)), dma((1,)), dma((2,)), dma((2,)),
         dma((dp - 1, 3)), dma((dp - 1, 3)), dma((3,)),
-        dma((dp - 1,)), dma((dp - 1,)), dma((1,)), dma((dp - 1,)), dma((dp - 1,)),
-        dma((chips,)), dma((chips,)), dma((chips,)), dma((n,)), dma((n - 1,)), dma((n - 1,)),
+        dma((dp - 1,)), dma((dp - 1,)),
+        dma((chips,)), dma((chips,)), dma((chips,)), dma((n,)), dma((n,)), dma((n,)),
         dma((chips,)), dma((chips,)), dma((chips,)), dma((chips,)),
     ]
     here, there = pl.BlockSpec(memory_space=pltpu.VMEM), pl.BlockSpec(memory_space=pl.ANY)
@@ -485,7 +505,7 @@
             jax.ShapeDtypeStruct((3 * seg_dev, width), BF),
             jax.ShapeDtypeStruct((3 * seg_dev, rows), BF),
         ),
-        in_specs=[there, here, here, there, there, there, there, there],
+        in_specs=[there, here, here, there, there, there, here, there],
         out_specs=(here, here),
         scratch_shapes=scratch,
         compiler_params=pltpu.CompilerParams(

time: 52.8 us -> 55.9 us (1.059)
  Pallas kernels: 50 us -> 53.2 us
    pallas_call x1, Pallas kernels: 50 us -> 53.2 us  [per_device(): pl.pallas_call(functools.partial(kernel, n, dp), out_shape=(jax.ShapeDtyp...]
where the time goes in v5:
time: 55.9 us; the launch traced here: 55.7 us
  Pallas kernels  53.2 us (95%)
  matrix products  2.54 us (5%)
    pallas_call x1, Pallas kernels, per_device(): pl.pallas_call(functools.partial(kernel, n, dp), out_shape=(jax.ShapeDtyp...  53.2 us
    dot_general x1, matrix products, dot(): lax.dot_general(left, right, ((dims[0], dims[1]), ((), ())), preferred_el...  2.54 us

profile of v5, /device:TPU:1, one launch (start us, length us, event | category | flops | bytes accessed | tf_op | source)
XLA Modules:
  0.0 55.7 jit_solution(18240592971379129362)
XLA Ops:
  0.0 0.0 copy-start
  0.0 53.2 %shard_map.82 = (bf16[192,1024]{1,0:T(8,128)(2,1)}, bf16[192,512]{1,0:T(8,128)(2,1)}) custom-call(bf16[1,512,1024]{2,1,0:T(8,128)(2,1)} %tok_hbm.1, s32[1,64]{1,0:T(1,128)} %starts.1, f32[1,1024]{1,0:T(1,128)} %bitcast.8, bf16[256,1024]{1,0:T(8,128)(2,1)} %wq.1, bf16[256,1024]{1,0:T(8,128)(2,1)} %wk.1, bf16[256,1024]{1,0:T(8,128)(2,1)} %wv.1, ...), custom_call_target="tpu_custom_call" | custom-call | tf_op jit(solution)/shard_map/pallas_call | solution.py:502
  53.2 0.0 copy-done
  53.2 2.5 %fusion.1 = bf16[1,512,1024]{2,1,0:T(8,128)(2,1)} fusion(bf16[192,512]{1,0:T(8,128)(2,1)} %get-tuple-element.7, bf16[192,1024]{1,0:T(8,128)(2,1)} %get-tuple-element.8, bf16[1,512,1024]{2,1,0:T(8,128)(2,1)S(1)} %copy-done), kind=kOutput, calls=%fused_computation.2 | convolution fusion | flops 202899456 | bytes 2686976 | tf_op jit(solution)/shard_map/dot_general | solution.py:17
Async XLA Ops:
  0.0 53.2 %copy-start = (bf16[1,512,1024]{2,1,0:T(8,128)(2,1)S(1)}, bf16[1,512,1024]{2,1,0:T(8,128)(2,1)}, u32[]{:S(2)}) copy-start(bf16[1,512,1024]{2,1,0:T(8,128)(2,1)} %cot_hbm.1) | copy-start | bytes 3145732

commit v6 on v2

--- a/solution.py
+++ b/solution.py
@@ -43,7 +43,7 @@
     qkv, dqkv, dkv, part, sib, red, rs, seg_out, seg_in,
     in_sem, st_send, st_recv, near_send, near_recv, head_send, head_recv, seg_send, seg_recv,
     w_send, w_recv, w_local, wo_send, wo_recv, wo_local, wo_fsend, wo_frecv,
-    right_send, left_send, pair_send, gath_recv, datt_send, datt_recv,
+    chip_send, pair_send, gath_recv, datt_send, datt_recv,
     sib_send, sib_recv, rs_send, rs_recv,
 ):
     me = lax.axis_index("dp")
@@ -218,51 +218,32 @@
         at = 2 * src_chip + core
         return remote(spot(at), spot(at), sems.at[src_chip], gath_recv.at[at], **where)
 
-    def go_right(src):
-        return hop(src, right_send, ctx=c + 2)
-
-    def go_left(src):
-        return hop(src, left_send, ctx=c - 2)
+    def go_chip(o):
+        to = lax.rem(chip + o, chips)
+        return remote(spot(c), spot(c), chip_send.at[o - 1], gath_recv.at[c], ctx=2 * to + core)
 
     def go_pair(src):
         return hop(src, pair_send, ctx=mate)
 
     def arrival(where):
-        return remote(spot(where), spot(where), right_send.at[0], gath_recv.at[where], ctx=mate)
-
-    not_last, not_first = chip < chips - 1, chip > 0
+        return remote(spot(where), spot(where), pair_send.at[0], gath_recv.at[where], ctx=mate)
+
     own_at = pl.ds(pl.multiple_of(c * seg_dev, seg_dev), seg_dev)
     gath[own_at] = (normed * gain[...]).astype(BF)
 
-    @pl.when(not_last)
-    def _():
-        go_right(chip).start()
-
-    @pl.when(not_first)
-    def _():
-        go_left(chip).start()
-
+    for o in range(1, chips):
+        go_chip(o).start()
     go_pair(chip).start()
 
     def relay(s):
         @pl.when(chip - s >= 0)
         def _():
             arrival(c - 2 * s).wait_recv()
-
-            @pl.when(not_last)
-            def _():
-                go_right(chip - s).start()
-
             go_pair(chip - s).start()
 
         @pl.when(chip + s < chips)
         def _():
             arrival(c + 2 * s).wait_recv()
-
-            @pl.when(not_first)
-            def _():
-                go_left(chip + s).start()
-
             go_pair(chip + s).start()
 
     def datt_copy(o):
@@ -390,16 +371,10 @@
     push(0)
 
     for other in range(chips):
-        @pl.when(not_last & (other <= chip))
-        def _():
-            go_right(other).wait_send()
-
-        @pl.when(not_first & (other >= chip))
-        def _():
-            go_left(other).wait_send()
-
         go_pair(other).wait_send()
         sib_copy(other).wait_send()
+    for o in range(1, chips):
+        go_chip(o).wait_send()
     for o in range(1, dp):
         for i in range(3):
             w_copy(o, i).wait_send()
@@ -475,7 +450,7 @@
         dma((2,)), dma((2,)), dma((2,)), dma((2, 2)), dma((2, 2)), dma((1,)), dma((1,)), dma((2,)), dma((2,)),
         dma((dp - 1, 3)), dma((dp - 1, 3)), dma((3,)),
         dma((dp - 1,)), dma((dp - 1,)), dma((1,)), dma((dp - 1,)), dma((dp - 1,)),
-        dma((chips,)), dma((chips,)), dma((chips,)), dma((n,)), dma((n - 1,)), dma((n - 1,)),
+        dma((chips,)), dma((chips,)), dma((n,)), dma((n - 1,)), dma((n - 1,)),
         dma((chips,)), dma((chips,)), dma((chips,)), dma((chips,)),
     ]
     here, there = pl.BlockSpec(memory_space=pltpu.VMEM), pl.BlockSpec(memory_space=pl.ANY)

time: 52.8 us -> 55.5 us (1.051)
  Pallas kernels: 50 us -> 52.8 us
    pallas_call x1, Pallas kernels: 50 us -> 52.8 us  [per_device(): pl.pallas_call(functools.partial(kernel, n, dp), out_shape=(jax.ShapeDtyp...]
where the time goes in v6:
time: 55.5 us; the launch traced here: 55.4 us
  Pallas kernels  52.8 us (95%)
  matrix products  2.54 us (5%)
    pallas_call x1, Pallas kernels, per_device(): pl.pallas_call(functools.partial(kernel, n, dp), out_shape=(jax.ShapeDtyp...  52.8 us
    dot_general x1, matrix products, dot(): lax.dot_general(left, right, ((dims[0], dims[1]), ((), ())), preferred_el...  2.54 us

profile of v6, /device:TPU:1, one launch (start us, length us, event | category | flops | bytes accessed | tf_op | source)
XLA Modules:
  0.0 55.4 jit_solution(7227760767441903083)
XLA Ops:
  0.0 0.0 copy-start
  0.0 52.8 %shard_map.82 = (bf16[192,1024]{1,0:T(8,128)(2,1)}, bf16[192,512]{1,0:T(8,128)(2,1)}) custom-call(bf16[1,512,1024]{2,1,0:T(8,128)(2,1)} %tok_hbm.1, s32[1,64]{1,0:T(1,128)} %starts.1, f32[1,1024]{1,0:T(1,128)} %bitcast.8, bf16[256,1024]{1,0:T(8,128)(2,1)} %wq.1, bf16[256,1024]{1,0:T(8,128)(2,1)} %wk.1, bf16[256,1024]{1,0:T(8,128)(2,1)} %wv.1, ...), custom_call_target="tpu_custom_call" | custom-call | tf_op jit(solution)/shard_map/pallas_call | solution.py:457
  52.8 0.0 copy-done
  52.8 2.5 %fusion.1 = bf16[1,512,1024]{2,1,0:T(8,128)(2,1)} fusion(bf16[192,512]{1,0:T(8,128)(2,1)} %get-tuple-element.7, bf16[192,1024]{1,0:T(8,128)(2,1)} %get-tuple-element.8, bf16[1,512,1024]{2,1,0:T(8,128)(2,1)S(1)} %copy-done), kind=kOutput, calls=%fused_computation.2 | convolution fusion | flops 202899456 | bytes 2686976 | tf_op jit(solution)/shard_map/dot_general | solution.py:17
Async XLA Ops:
  0.0 52.8 %copy-start = (bf16[1,512,1024]{2,1,0:T(8,128)(2,1)S(1)}, bf16[1,512,1024]{2,1,0:T(8,128)(2,1)}, u32[]{:S(2)}) copy-start(bf16[1,512,1024]{2,1,0:T(8,128)(2,1)} %cot_hbm.1) | copy-start | bytes 3145732
